TPU v7x, 32 devices: a whole 2x2x4 slice. The times are simulated.
32 devices in a mesh: front: 2 (over core), row: 4 (over y, x), col: 4 (over z).
Axes of the slice: x: 2, y: 2, z: 4, core: 2. Of those that a mesh axis runs over, the one named last changes fastest.
Arguments:
- front_block: float32 [2, 8192, 8192], P('front', 'row', 'col'), as said below
- child_tiles: float32 [2, 224, 16, 128], P('front', ('row', 'col')), may hold values from -3 to 3
- child_rows: int32 [2, 224, 16], P('front', ('row', 'col')), may hold values from 0 to 2047
- child_cols: int32 [2, 224, 128], P('front', ('row', 'col')), may hold values from 0 to 2047
- child_owner: int32 [2, 224], P('front', ('row', 'col')), may hold values from 0 to 15, as said below
Outputs:
- updated_front: float32 [2, 8192, 8192], P('front', 'row', 'col')
Inputs may be any that keep to these rules, and one draw needn't show every extreme that they name: `child_owner`: among the tiles of one device no owner appears more than 2 times; in every front some owner gets exactly 2 tiles from every device. `front_block`: the leading 1024 x 1024 block of each assembled front has a symmetric part that is positive definite.
All inputs are finite; a program needn't handle non-finite values.
Results may differ from a plain program's by a relative error of at most 0.0001.
Values sent between devices are 32-bit elements; how exact they have to be, the bound alone decides.
No kernel may reach another device: no remote copies, remote signals or barrier semaphores. Data moves between devices by JAX's collectives and lax.ppermute only.
A program may use at most 256 MiB of HBM per device.

v0:
```python
import jax
import jax.numpy as jnp
from jax import lax
from jax.sharding import PartitionSpec as P

P_SIZE = 1024
DB = 128
CR = 16
CC = 128
CAP = 2


def spread(array, axis, root):
    mine = lax.axis_index(axis) == root
    return lax.psum(jnp.where(mine, array, jnp.zeros_like(array)), axis)


def blocked_factor(symmetric):
    count = symmetric.shape[0] // DB
    remaining = symmetric
    columns = []
    inverses = []
    identity = jnp.eye(DB, dtype=symmetric.dtype)
    for step in range(count):
        start = step * DB
        chol = jnp.linalg.cholesky(remaining[:DB, :DB])
        inverse = lax.linalg.triangular_solve(chol, identity, left_side=True, lower=True)
        below = jnp.dot(remaining[DB:, :DB], inverse.T, precision=lax.Precision.HIGHEST)
        remaining = remaining[DB:, DB:] - jnp.dot(below, below.T, precision=lax.Precision.HIGHEST)
        columns.append(jnp.concatenate([jnp.zeros((start, DB), symmetric.dtype), chol, below], 0))
        inverses.append(inverse)
    return (jnp.concatenate(columns, 1), inverses)


def blocked_solve(panel, factor, inverses):
    solved_parts = []
    for step in range(len(inverses)):
        start = step * DB
        rhs = panel[:, start : start + DB]
        if step > 0:
            earlier = jnp.concatenate(solved_parts, 1)
            rhs = rhs - jnp.dot(
                earlier, factor[start : start + DB, :start].T, precision=lax.Precision.HIGHEST
            )
        solved_parts.append(jnp.dot(rhs, inverses[step].T, precision=lax.Precision.HIGHEST))
    return jnp.concatenate(solved_parts, 1)


def local(front_block, child_tiles, child_rows, child_cols, child_owner):
    front_part = front_block[0]
    child_part = child_tiles[0]
    row_maps = child_rows[0]
    col_maps = child_cols[0]
    owners = child_owner[0]
    row_count = lax.axis_size("row")
    col_count = lax.axis_size("col")
    group_count = row_count * col_count
    block_rows, block_cols = front_part.shape
    tile_count = owners.shape[0]
    positions = jnp.arange(tile_count)
    earlier = (owners[:, None] == owners[None, :]) & (positions[None, :] < positions[:, None])
    tile_rank = jnp.sum(earlier.astype(jnp.int32), axis=1)
    slot_index = owners * CAP + tile_rank
    send_tiles = (
        jnp.zeros((group_count * CAP, CR, CC), front_part.dtype).at[slot_index].set(child_part)
    )
    send_rows = jnp.zeros((group_count * CAP, CR), jnp.int32).at[slot_index].set(row_maps)
    send_cols = jnp.zeros((group_count * CAP, CC), jnp.int32).at[slot_index].set(col_maps)
    recv_tiles, recv_rows, recv_cols = (
        lax.all_to_all(send_tiles, ("row", "col"), split_axis=0, concat_axis=0, tiled=True),
        lax.all_to_all(send_rows, ("row", "col"), split_axis=0, concat_axis=0, tiled=True),
        lax.all_to_all(send_cols, ("row", "col"), split_axis=0, concat_axis=0, tiled=True),
    )
    assembled = front_part.at[recv_rows[:, :, None], recv_cols[:, None, :]].add(recv_tiles)
    panel_block = spread(assembled[:, :P_SIZE], "col", 0)
    row_index = lax.axis_index("row")
    col_index = lax.axis_index("col")
    first_row = row_index * block_rows
    held_rows = min(P_SIZE, block_rows)
    holders = max(1, P_SIZE // block_rows)
    diag_pieces = [spread(panel_block[:held_rows], "row", member) for member in range(holders)]
    diag_block = jnp.concatenate(diag_pieces, 0)
    symmetric = 0.5 * (diag_block + diag_block.T)
    factor, inverses = blocked_factor(symmetric)
    solved = blocked_solve(panel_block, factor, inverses)
    global_rows = first_row + jnp.arange(block_rows)
    below_mask = global_rows[:, None] >= P_SIZE
    if block_rows <= P_SIZE:
        factor_rows = lax.dynamic_slice_in_dim(
            factor, jnp.minimum(first_row, P_SIZE - block_rows), block_rows, 0
        )
    else:
        factor_rows = jnp.concatenate(
            [factor, jnp.zeros((block_rows - P_SIZE, P_SIZE), factor.dtype)], 0
        )
    panel_out = jnp.where(below_mask, solved, factor_rows)
    lower_part = jnp.where(below_mask, solved, 0.0)
    group_ratio = row_count // col_count
    column_parts = [
        spread(lower_part, "row", col_index * group_ratio + member) for member in range(group_ratio)
    ]
    column_part = jnp.concatenate(column_parts, 0)
    schur_block = assembled - jnp.dot(lower_part, column_part.T, precision=lax.Precision.HIGHEST)
    global_cols = col_index * block_cols + jnp.arange(block_cols)
    left_part = jnp.concatenate(
        [panel_out, jnp.zeros((block_rows, block_cols - P_SIZE), panel_out.dtype)], 1
    )
    trailing = below_mask & (global_cols[None, :] >= P_SIZE)
    updated = jnp.where(
        global_cols[None, :] < P_SIZE, left_part, jnp.where(trailing, schur_block, assembled)
    )
    return updated[None]


def solution(mesh):
    placed = (
        P("front", "row", "col"),
        P("front", ("row", "col"), None, None),
        P("front", ("row", "col"), None),
        P("front", ("row", "col"), None),
        P("front", ("row", "col")),
    )
    return jax.shard_map(
        local, mesh=mesh, in_specs=placed, out_specs=P("front", "row", "col"), check_vma=False
    )
```

profile of v0, /device:TPU:12, one launch (start us, length us, event | category | flops | bytes accessed | tf_op | source)
XLA Modules:
  0.0 1547.2 jit_solution(17233238175195343713)
XLA Ops:
  9.5 7.2 all-to-all-start
  16.7 14.2 copy.84
  34.9 6.9 all-to-all-start.1
  41.9 5.1 all-to-all-done.1
  47.0 5.7 all-to-all-start.2
  53.1 6.6 all-to-all-done.2
  59.7 410.7 %scatter_fusion.1 = f32[4194304]{0:T(1024)} fusion(f32[4194304]{0:T(1024)} %bitcast.145, s32[65536]{0:T(1024)S(1)} %bitcast.150, f32[65536]{0:T(1024)S(1)} %bitcast.149), kind=kCustom, calls=%fused_computation.3 | custom fusion | flops 65536 | bytes 1048576
  470.5 18.0 %reshape.91 = f32[2048,2048]{1,0:T(8,128)} reshape(f32[4194304]{0:T(1024)} %scatter_fusion.1) | data formatting | bytes 33554432 | tf_op jit(solution)/shard_map/scatter-add | solution.py:74
  488.5 8.7 slice_select_fusion
  497.2 328.7 %all-reduce.7.cloned.1.call-done = f32[2048,1024]{1,0:T(8,128)} async-done(((f32[2048,1024]{1,0:T(8,128)}), f32[2048,1024]{1,0:T(8,128)}) %all-reduce.7.cloned.1.call-update) | async-done | bytes 8388624 | tf_op jit(solution)/shard_map/psum | solution.py:15
  825.9 5.0 slice_select_fusion.1
  831.1 104.7 %all-reduce.9.cloned.1.call-done = f32[1024,1024]{1,0:T(8,128)} async-done(((f32[1024,1024]{1,0:T(8,128)}), f32[1024,1024]{1,0:T(8,128)}) %all-reduce.9.cloned.1.call-update) | async-done | bytes 4194320 | tf_op jit(solution)/shard_map/psum | solution.py:15
  935.8 5.8 copy.56
  941.6 4.4 fusion.14
  949.2 11.7 cholesky.134
  962.2 9.8 custom-call.12
  973.9 4.1 constant_dynamic-update-slice_fusion.17
  979.4 5.0 slice_subtract_fusion
  987.2 11.7 cholesky.145
  1000.1 9.8 custom-call.13
  1011.7 3.1 convolution_subtract_fusion.4
  1014.8 2.9 constant_dynamic-update-slice_fusion.16
  1019.0 3.9 slice_subtract_fusion.1
  1025.4 11.7 cholesky.156
  1039.1 9.8 custom-call.14
  1052.2 4.8 convolution_subtract_fusion.3
  1057.0 3.2 constant_dynamic-update-slice_fusion.15
  1062.7 3.3 slice_subtract_fusion.2
  1068.3 11.7 cholesky.167
  1081.9 9.8 custom-call.15
  1093.4 7.1 fusion.23
  1100.5 3.2 constant_dynamic-update-slice_fusion.14
  1114.7 13.2 cholesky.178
  1131.6 11.3 custom-call.16
  1146.0 9.0 fusion.26
  1155.1 2.9 constant_dynamic-update-slice_fusion.13
  1160.2 11.7 cholesky.189
  1173.2 10.0 custom-call.17
  1191.8 10.7 convolution_subtract_fusion.2
  1207.9 11.7 cholesky.200
  1221.7 9.8 custom-call.18
  1233.5 12.5 convolution_subtract_fusion
  1249.8 11.7 cholesky.211
  1263.0 9.8 custom-call.19
  1280.5 15.0 convolution_subtract_fusion.1
  1296.5 7.1 select_select_fusion
  1304.8 172.2 %all-reduce.11.cloned.1.call-done = f32[2048,1024]{1,0:T(8,128)} async-done(((f32[2048,1024]{1,0:T(8,128)}), f32[2048,1024]{1,0:T(8,128)}) %all-reduce.11.cloned.1.call-update) | async-done | bytes 8388624 | tf_op jit(solution)/shard_map/psum | solution.py:15
  1477.0 63.5 %fusion.1 = f32[1,2048,2048]{2,1,0:T(8,128)} fusion(f32[2048,2048]{1,0:T(8,128)} %reshape.91, f32[2048,1024]{1,0:T(8,128)} %get-tuple-element.24, pred[2048]{0:T(1024)(128)(4,1)S(1)} %get-tuple-element.75, pred[2048]{0:T(1024)(128)(4,1)S(1)} %get-tuple-element.76, pred[2048]{0:T(1024)(128)(4,1)S(1)} %add_compare_fusion, ...), kind=kOutput, calls=%fused_computation.6 | convolution fusion | flops 51558481920 | bytes 58726400 | tf_op jit(solution)/shard_map/dot_general | solution.py:103
  (193 shorter events, 92.7 us)
Async XLA Ops:
  9.5 25.5 %all-to-all-start = ((s32[16,2,16]{2,1,0:T(2,128)}), s32[16,2,16]{2,1,0:T(2,128)S(1)}, u32[]{:S(2)}, u32[]{:S(2)}) async-start(s32[16,2,16]{2,1,0:T(2,128)} %bitcast.4), calls=%async_computation | async-start | bytes 32768 | tf_op jit(solution)/shard_map/all_to_all | solution.py:71
  16.6 14.3 copy-start.27
  16.6 16.1 %copy-start.26 = (f32[1,14,16,128]{3,2,1,0:T(8,128)S(1)}, f32[1,14,16,128]{3,2,1,0:T(8,128)}, u32[]{:S(2)}) copy-start(f32[1,14,16,128]{3,2,1,0:T(8,128)} %param.9) | copy-start | bytes 344068
  16.6 36.3 %copy-start.28 = (s32[2]{0:T(128)S(1)}, s32[2]{0:T(128)}, u32[]{:S(2)}) copy-start(s32[2]{0:T(128)} %constant.79) | copy-start | bytes 28
  34.9 12.0 all-to-all-start.1
  47.0 12.7 all-to-all-start.2
  52.6 773.3 %all-reduce.7.cloned.1.call-start = ((), (), s32[]{:S(2)}) async-start(), calls=%async_computation.3 | async-start | bytes 16777216 | tf_op jit(solution)/shard_map/psum | solution.py:15
  497.2 438.6 %all-reduce.9.cloned.1.call-start = ((), (), s32[]{:S(2)}) async-start(), calls=%async_computation.4 | async-start | bytes 8388608 | tf_op jit(solution)/shard_map/psum | solution.py:15
  831.0 646.0 %all-reduce.11.cloned.1.call-start = ((), (), s32[]{:S(2)}) async-start(), calls=%async_computation.5 | async-start | bytes 16777216 | tf_op jit(solution)/shard_map/psum | solution.py:15
  946.0 2.1 copy-start
  962.2 90.0 %copy-start.19 = (f32[128,128]{1,0:T(8,128)}, f32[128,128]{1,0:T(8,128)S(1)}, u32[]{:S(2)}) copy-start(f32[128,128]{1,0:T(8,128)S(1)} %get-tuple-element.22) | copy-start | bytes 196612
  984.4 1.7 copy-start.1
  1000.1 52.1 %copy-start.18 = (f32[128,128]{1,0:T(8,128)}, f32[128,128]{1,0:T(8,128)S(1)}, u32[]{:S(2)}) copy-start(f32[128,128]{1,0:T(8,128)S(1)} %get-tuple-element.20) | copy-start | bytes 196612
  1022.9 1.4 copy-start.3
  1052.2 8.0 copy-start.20
  1066.0 1.2 copy-start.4
  1093.4 10.3 copy-start.16
  1108.5 1.0 copy-start.12
  1146.0 9.0 copy-start.21
  1155.0 4.2 copy-start.13
  1155.1 4.2 copy-start.14
  1158.0 28.3 %copy-start.17 = (f32[256,128]{1,0:T(8,128)S(1)}, f32[256,128]{1,0:T(8,128)}, u32[]{:S(2)}) copy-start(f32[256,128]{1,0:T(8,128)} %copy-done.16) | copy-start | bytes 393220
  1159.3 29.3 %copy-start.22 = (f32[384,128]{1,0:T(8,128)S(1)}, f32[384,128]{1,0:T(8,128)}, u32[]{:S(2)}) copy-start(f32[384,128]{1,0:T(8,128)} %copy-done.21) | copy-start | bytes 589828
  1159.3 29.3 %copy-start.23 = (f32[128,128]{1,0:T(8,128)S(1)}, f32[128,128]{1,0:T(8,128)}, u32[]{:S(2)}) copy-start(f32[128,128]{1,0:T(8,128)} %get-tuple-element.16) | copy-start | bytes 196612
  1159.9 30.2 %copy-start.15 = (f32[384,384]{1,0:T(8,128)}, f32[384,384]{1,0:T(8,128)S(1)}, u32[]{:S(2)}) copy-start(f32[384,384]{1,0:T(8,128)S(1)} %convolution_subtract_fusion.6) | copy-start | bytes 1769476
  1173.2 16.9 %copy-start.24 = (f32[128,128]{1,0:T(8,128)S(1)}, f32[128,128]{1,0:T(8,128)}, u32[]{:S(2)}) copy-start(f32[128,128]{1,0:T(8,128)} %get-tuple-element.14) | copy-start | bytes 196612
  1246.0 27.1 %copy-start.6 = (f32[2048,128]{1,0:T(8,128)S(1)}, f32[2048,128]{1,0:T(8,128)}, u32[]{:S(2)}) copy-start(f32[2048,128]{1,0:T(8,128)} %copy.74) | copy-start | bytes 3145732
  1246.0 28.2 %copy-start.7 = (f32[2048,128]{1,0:T(8,128)S(1)}, f32[2048,128]{1,0:T(8,128)}, u32[]{:S(2)}) copy-start(f32[2048,128]{1,0:T(8,128)} %copy.75) | copy-start | bytes 3145732
  1249.3 25.9 %copy-start.8 = (f32[2048,128]{1,0:T(8,128)S(1)}, f32[2048,128]{1,0:T(8,128)}, u32[]{:S(2)}) copy-start(f32[2048,128]{1,0:T(8,128)} %copy.76) | copy-start | bytes 3145732
  1272.8 3.5 copy-start.9
  1273.1 4.2 copy-start.10
  1274.1 4.2 copy-start.11
  1275.2 4.2 copy-start.5
  1275.2 4.2 copy-start.25
  1280.4 15.1 slice-start
  1280.5 15.0 slice-start.1
  1296.5 8.3 copy-start.2
Sparse Core Ops, SparseCore 0:
  497.3 328.5 all-reduce.6
  831.1 104.6 all-reduce.8
  1304.9 172.0 all-reduce.10
where the time goes:
time: 1560 us; the launch traced here: 1550 us
  other arithmetic  645 us (41%)
  waiting for transfers between devices  617 us (40%)
  matrix products  175 us (11%)
  local copies, waits for them, and re-layouts  75.3 us (5%)
  starting transfers between devices  19.9 us (1%)
    psum x3, waiting for transfers between devices, spread(): return lax.psum(jnp.where(mine, array, jnp.zeros_like(array)), axis)  606 us
    unnamed x12, other arithmetic  423 us
    another operation x24, other arithmetic, blocked_factor(): chol = jnp.linalg.cholesky(remaining[:DB, :DB])  102 us
    another operation x16, other arithmetic, blocked_factor(): lax.linalg.triangular_solve(chol, identity, left_side=True, lower=True)  88.6 us
    dot_general x1, matrix products, local(): jnp.dot(lower_part, column_part.T, precision=lax.Precision.HIGHEST)  63.5 us
    dot_general x7, matrix products, blocked_solve(): jnp.dot(earlier, factor[start:start + DB, :start].T, precision=lax.Precis...  62.2 us
  transfers between devices with their start and end apart: 6, of which 5 were waited for; matrix products, arithmetic and copies ran while one was open for 1% of the time, Pallas kernels for 0%

commit v1 on v0

--- a/solution.py
+++ b/solution.py
@@ -1,6 +1,9 @@
+import functools
 import jax
 import jax.numpy as jnp
 from jax import lax
+from jax.experimental import pallas as pl
+from jax.experimental.pallas import tpu as pltpu
 from jax.sharding import PartitionSpec as P
 
 P_SIZE = 1024
@@ -8,11 +11,436 @@
 CR = 16
 CC = 128
 CAP = 2
+GROUP = 8
+WIDE = 512
+SLOT = 24
+CHUNKS = 8
+STRIP = 256
+MIB = 2**20
+GRID = ("row", "col")
+HIGHEST = lax.Precision.HIGHEST
+VMEM = pltpu.VMEM
+F32 = jnp.float32
+BF16 = jnp.bfloat16
 
 
 def spread(array, axis, root):
     mine = lax.axis_index(axis) == root
     return lax.psum(jnp.where(mine, array, jnp.zeros_like(array)), axis)
+
+
+def of_lane(tile, at):
+    return jnp.broadcast_to(tile[:, at : at + 1], tile.shape)
+
+
+def of_row(tile, at):
+    return jnp.broadcast_to(tile[at : at + 1, :], tile.shape)
+
+
+def reciprocal(value):
+    guess = pl.reciprocal(value, approx=True)
+    guess = guess * (2.0 - value * guess)
+    return guess * (2.0 - value * guess)
+
+
+def tree_sum(terms):
+    while len(terms) > 1:
+        terms = [terms[at] + terms[at + 1] for at in range(0, len(terms), 2)]
+    return terms[0]
+
+
+def factor_tile(w):
+    n = DB // GROUP
+    row = lax.broadcasted_iota(jnp.int32, (GROUP, DB), 0)
+    col = lax.broadcasted_iota(jnp.int32, (GROUP, DB), 1)
+    x = [jnp.where(col == row + GROUP * i, 1.0, 0.0).astype(F32) for i in range(n)]
+    upper, inverse = [], []
+    for g in range(n):
+        first = GROUP * g
+        lanes = [of_lane(w[g], first + m) for m in range(GROUP)]
+        s = {(k, m): of_row(lanes[m], k) for m in range(GROUP) for k in range(m + 1)}
+        rw = [of_row(w[g], k) for k in range(GROUP)]
+        rx = [of_row(x[g], k) for k in range(GROUP)]
+        l, rec = {}, []
+        for k in range(GROUP):
+            rec.append(reciprocal(s[k, k]))
+            for i in range(k + 1, GROUP):
+                l[i, k] = s[k, i] * rec[k]
+            for i in range(k + 1, GROUP):
+                for m in range(i, GROUP):
+                    s[i, m] = s[i, m] - l[i, k] * s[k, m]
+                rw[i] = rw[i] - l[i, k] * rw[k]
+                rx[i] = rx[i] - l[i, k] * rx[k]
+        scale = [lax.rsqrt(s[k, k]) for k in range(GROUP)]
+        up, inv = rw[0] * scale[0], rx[0] * scale[0]
+        for k in range(1, GROUP):
+            up = jnp.where(row == k, rw[k] * scale[k], up)
+            inv = jnp.where(row == k, rx[k] * scale[k], inv)
+        upper.append(jnp.where(col >= row + first, up, 0.0))
+        inverse.append(inv)
+        if g + 1 == n:
+            break
+        qw = [rw[k] * rec[k] for k in range(GROUP)]
+        qx = [rx[k] * rec[k] for k in range(GROUP)]
+        for k in reversed(range(GROUP)):
+            for i in range(k):
+                qw[i] = qw[i] - l[k, i] * qw[k]
+                qx[i] = qx[i] - l[k, i] * qx[k]
+        for i in range(g + 1, n):
+            at = [of_lane(w[i], first + m) for m in range(GROUP)]
+            w[i] = w[i] - tree_sum([at[m] * qw[m] for m in range(GROUP)])
+            x[i] = x[i] - tree_sum([at[m] * qx[m] for m in range(GROUP)])
+    return upper, inverse
+
+
+def dot(a, b, dims=((1,), (0,))):
+    return lax.dot_general(a, b, (dims, ((), ())), precision=HIGHEST, preferred_element_type=F32)
+
+
+NT = ((1,), (1,))
+TN = ((0,), (0,))
+
+
+def factor_kernel(blocks, a_ref, l_ref, z_ref, u_ref, d_ref):
+    def block(i):
+        return pl.ds(pl.multiple_of(i * DB, DB), DB)
+
+    def symmetric(i, _):
+        def one(j, _):
+            z_ref[block(i), block(j)] = 0.5 * (a_ref[block(i), block(j)] + a_ref[block(j), block(i)].T)
+            return 0
+
+        lax.fori_loop(0, blocks, one, 0)
+        return 0
+
+    lax.fori_loop(0, blocks, symmetric, 0)
+
+    def step(j, _):
+        now = block(j)
+        base = pl.multiple_of(j * DB, DB)
+        tiles = [
+            z_ref[pl.ds(pl.multiple_of(base + GROUP * i, GROUP), GROUP), now]
+            for i in range(DB // GROUP)
+        ]
+        upper, inverse = factor_tile(tiles)
+        for i in range(DB // GROUP):
+            u_ref[GROUP * i : GROUP * i + GROUP, now] = upper[i]
+            d_ref[GROUP * i : GROUP * i + GROUP, :] = inverse[i]
+            z_ref[pl.ds(pl.multiple_of(base + GROUP * i, GROUP), GROUP), now] = inverse[i]
+        m = d_ref[...]
+        l_ref[now, now] = u_ref[:, now].T
+        for c in range(0, blocks * DB, WIDE):
+            u_ref[:, c : c + WIDE] = dot(m, z_ref[now, c : c + WIDE])
+        u_ref[:, now] = m
+        z_ref[now, :] = u_ref[...]
+
+        def trail(i, _):
+            below = block(i)
+            ui = u_ref[:, below]
+            l_ref[below, now] = ui.T
+            l_ref[now, below] = jnp.zeros((DB, DB), F32)
+            z_ref[below, now] = jnp.zeros((DB, DB), F32)
+            for c in range(0, blocks * DB, WIDE):
+                z_ref[below, c : c + WIDE] = z_ref[below, c : c + WIDE] - dot(
+                    ui, u_ref[:, c : c + WIDE], TN
+                )
+            return 0
+
+        lax.fori_loop(j + 1, blocks, trail, 0)
+        return 0
+
+    lax.fori_loop(0, blocks, step, 0)
+
+    def clean(i, _):
+        def one(j, _):
+            z_ref[block(i), block(j)] = jnp.zeros((DB, DB), F32)
+            return 0
+
+        lax.fori_loop(i + 1, blocks, one, 0)
+        return 0
+
+    lax.fori_loop(0, blocks, clean, 0)
+
+
+def maybe_factor_kernel(blocks, holds_ref, a_ref, *rest):
+    @pl.when(holds_ref[0] == 1)
+    def _():
+        factor_kernel(blocks, a_ref, *rest)
+
+
+def factor(block, holds):
+    size = block.shape[0]
+    return pl.pallas_call(
+        functools.partial(maybe_factor_kernel, size // DB),
+        out_shape=[jax.ShapeDtypeStruct((size, size), F32)] * 2,
+        in_specs=[pl.BlockSpec(memory_space=pltpu.SMEM), pl.BlockSpec(memory_space=VMEM)],
+        out_specs=[pl.BlockSpec(memory_space=VMEM)] * 2,
+        scratch_shapes=[VMEM((DB, size), F32), VMEM((DB, DB), F32)],
+        compiler_params=pltpu.CompilerParams(vmem_limit_bytes=40 * MIB),
+        name="panel_factor",
+    )(jnp.full((1,), holds, jnp.int32), block)
+
+
+def pack_kernel(groups, owner_ref, tile_ref, row_ref, col_ref, out_ref, seen_ref):
+    out_ref[...] = jnp.zeros_like(out_ref)
+    for group in range(groups):
+        seen_ref[group] = 0
+
+    def place(t, _):
+        owner = owner_ref[t]
+        rank = seen_ref[owner]
+        seen_ref[owner] = rank + 1
+        slot = owner * CAP + rank
+        out_ref[slot, 0:CR, :] = tile_ref[t]
+        out_ref[slot, CR : CR + 1, :] = col_ref[t].astype(F32)
+        out_ref[slot, CR + 1 : CR + 2, :] = row_ref[t].astype(F32)
+        return 0
+
+    lax.fori_loop(0, tile_ref.shape[0], place, 0)
+
+
+def pack(tiles, rows, cols, owners, groups):
+    count = owners.shape[0]
+    rows = jnp.pad(rows, ((0, 0), (0, CC - CR))).reshape(count, 1, CC)
+    return pl.pallas_call(
+        functools.partial(pack_kernel, groups),
+        out_shape=jax.ShapeDtypeStruct((groups * CAP, SLOT, CC), F32),
+        in_specs=[pl.BlockSpec(memory_space=pltpu.SMEM)] + [pl.BlockSpec(memory_space=VMEM)] * 3,
+        out_specs=pl.BlockSpec(memory_space=VMEM),
+        scratch_shapes=[pltpu.SMEM((groups,), jnp.int32)],
+        name="pack_tiles",
+    )(owners, tiles, rows, cols.reshape(count, 1, CC))
+
+
+def halves(value):
+    high = value.astype(BF16)
+    return high, (value - high.astype(F32)).astype(BF16)
+
+
+def mm(a, b, dims):
+    return lax.dot_general(a, b, (dims, ((), ())), preferred_element_type=F32)
+
+
+def expand_kernel(slots_ref, high_ref, low_ref):
+    cols = high_ref.shape[0]
+    place = lax.broadcasted_iota(jnp.int32, (cols, 2 * CC), 0)
+    row = lax.broadcasted_iota(jnp.int32, (CC, CC), 0) // CR
+    total = jnp.zeros((cols, 2 * CC), F32)
+    for pair in range(0, 8, 2):
+        index = jnp.concatenate([slots_ref[pair + k, CR : CR + 1, :] for k in range(2)], 1)
+        onehot = jnp.where(place == index.astype(jnp.int32), 1.0, 0.0).astype(BF16)
+        highs, lows = [], []
+        for k in range(2):
+            tile = slots_ref[pair + k, 0:CR, :]
+            tall = jnp.concatenate([tile] * (CC // CR), 0)
+            high, low = halves(jnp.where(row == pair + k, tall, 0.0))
+            highs.append(high)
+            lows.append(low)
+        packed = jnp.concatenate([jnp.concatenate(highs, 1), jnp.concatenate(lows, 1)], 0)
+        total = total + mm(onehot, packed, NT)
+    high, low = halves(total[:, :CC] + total[:, CC:])
+    high_ref[...] = high
+    low_ref[...] = low
+
+
+def expand(slots, cols):
+    count = slots.shape[0]
+    return pl.pallas_call(
+        expand_kernel,
+        grid=(count // 8,),
+        out_shape=[jax.ShapeDtypeStruct((cols, count * CR), BF16)] * 2,
+        in_specs=[pl.BlockSpec((8, SLOT, CC), lambda g: (g, 0, 0))],
+        out_specs=[pl.BlockSpec((cols, CC), lambda g: (0, g))] * 2,
+        compiler_params=pltpu.CompilerParams(vmem_limit_bytes=40 * MIB),
+        name="expand_columns",
+    )(slots)
+
+
+def assemble_kernel(step, rows_ref, high_ref, low_ref, front_ref, out_ref):
+    first = pl.program_id(0) * step
+    place = lax.broadcasted_iota(jnp.int32, (step, rows_ref.shape[1]), 0) + first
+    onehot = jnp.where(place == rows_ref[...], 1.0, 0.0).astype(BF16)
+    out_ref[...] = front_ref[...] + (mm(onehot, high_ref[...], NT) + mm(onehot, low_ref[...], NT))
+
+
+def assemble(front, rows, high, low):
+    step = 256
+    count, width = front.shape
+    k = rows.shape[1]
+    return pl.pallas_call(
+        functools.partial(assemble_kernel, step),
+        grid=(count // step,),
+        out_shape=jax.ShapeDtypeStruct((count, width), F32),
+        in_specs=[
+            pl.BlockSpec((1, k), lambda i: (0, 0)),
+            pl.BlockSpec((width, k), lambda i: (0, 0)),
+            pl.BlockSpec((width, k), lambda i: (0, 0)),
+            pl.BlockSpec((step, width), lambda i: (i, 0)),
+        ],
+        out_specs=pl.BlockSpec((step, width), lambda i: (i, 0)),
+        compiler_params=pltpu.CompilerParams(vmem_limit_bytes=40 * MIB),
+        name="assemble",
+    )(rows, high, low, front)
+
+
+def solve_kernel(rows_ref, *refs):
+    strips = refs[: P_SIZE // STRIP]
+    out_high_ref, out_low_ref, high_ref, low_ref = refs[P_SIZE // STRIP :]
+
+    @pl.when(pl.program_id(0) == 0)
+    def _():
+        for i, strip in enumerate(strips):
+            c, upto = i * STRIP, (i + 1) * STRIP
+            high_ref[c:upto, :upto], low_ref[c:upto, :upto] = halves(strip[...])
+
+    for c in range(0, P_SIZE, STRIP):
+        upto = c + STRIP
+        a, b = halves(rows_ref[:, :upto])
+        high, low = high_ref[c:upto, :upto], low_ref[c:upto, :upto]
+        part = mm(a, high, NT) + (mm(a, low, NT) + mm(b, high, NT))
+        out_high_ref[:, c:upto], out_low_ref[:, c:upto] = halves(part)
+
+
+def solve(rows, strips):
+    step = min(512, rows.shape[0])
+    part = pl.BlockSpec((step, P_SIZE), lambda i: (i, 0))
+    return pl.pallas_call(
+        solve_kernel,
+        grid=(rows.shape[0] // step,),
+        out_shape=[jax.ShapeDtypeStruct(rows.shape, BF16)] * 2,
+        in_specs=[part] + [pl.BlockSpec(strip.shape, lambda i: (0, 0)) for strip in strips],
+        out_specs=[part, part],
+        scratch_shapes=[VMEM((P_SIZE, P_SIZE), BF16)] * 2,
+        compiler_params=pltpu.CompilerParams(vmem_limit_bytes=40 * MIB),
+        name="solve_rows",
+    )(rows, *strips)
+
+
+def update_kernel(step, place_ref, rh_ref, rl_ref, ch_ref, cl_ref, front_ref, factor_ref, out_ref):
+    above = (place_ref[0] == 0) & (pl.program_id(0) * step < P_SIZE)
+    first_col = place_ref[1] == 0
+    width = out_ref.shape[1]
+
+    def schur(left):
+        a, b = rh_ref[...], rl_ref[...]
+        for c in range(left, width, WIDE):
+            high, low = ch_ref[c : c + WIDE, :], cl_ref[c : c + WIDE, :]
+            part = mm(a, high, NT) + (mm(a, low, NT) + mm(b, high, NT))
+            out_ref[:, c : c + WIDE] = front_ref[:, c : c + WIDE] - part
+
+    @pl.when(above)
+    def _():
+        out_ref[...] = front_ref[...]
+
+        @pl.when(first_col)
+        def _():
+            out_ref[:, :P_SIZE] = factor_ref[...]
+
+    @pl.when(jnp.logical_not(above) & first_col)
+    def _():
+        out_ref[:, :P_SIZE] = rh_ref[...].astype(F32) + rl_ref[...].astype(F32)
+        schur(P_SIZE)
+
+    @pl.when(jnp.logical_not(above) & jnp.logical_not(first_col))
+    def _():
+        schur(0)
+
+
+def update(place, row_parts, col_parts, front, factor_rows):
+    step = 256
+    count, width = front.shape
+    row = pl.BlockSpec((step, P_SIZE), lambda i: (i, 0))
+    whole = pl.BlockSpec((width, P_SIZE), lambda i: (0, 0))
+    wide = pl.BlockSpec((step, width), lambda i: (i, 0))
+    last = P_SIZE // step - 1
+    return pl.pallas_call(
+        functools.partial(update_kernel, step),
+        grid=(count // step,),
+        out_shape=jax.ShapeDtypeStruct((count, width), F32),
+        in_specs=[
+            pl.BlockSpec(memory_space=pltpu.SMEM),
+            row,
+            row,
+            whole,
+            whole,
+            wide,
+            pl.BlockSpec((step, P_SIZE), lambda i: (jnp.minimum(i, last), 0)),
+        ],
+        out_specs=wide,
+        compiler_params=pltpu.CompilerParams(vmem_limit_bytes=56 * MIB),
+        name="schur_update",
+    )(place, *row_parts, *col_parts, front, factor_rows)
+
+
+def pairs_of(route, rows, cols, col_count):
+    return [
+        (r * col_count + c, to[0] * col_count + to[1])
+        for r in rows
+        for c in cols
+        for to in [route(r, c)]
+        if to is not None
+    ]
+
+
+def down_columns(part, col, rows):
+    moves = [[(r * 4 + a, r * 4 + b) for r in rows] for a, b in ((0, 2), (2, 1), (2, 3))]
+    middle = lax.ppermute(part, GRID, moves[0])
+    one = lax.ppermute(middle, GRID, moves[1])
+    three = lax.ppermute(middle, GRID, moves[2])
+    return jnp.where(col == 0, part, jnp.where(col == 2, middle, jnp.where(col == 1, one, three)))
+
+
+def in_plane(part, row, col, cols, source, hops):
+    held = part
+    result = part
+    at = 0
+    for hop in hops:
+        pairs = [((source(c) ^ at) * 4 + c, (source(c) ^ at ^ hop) * 4 + c) for c in cols]
+        held = lax.ppermute(held, GRID, pairs)
+        at ^= hop
+        result = jnp.where(row == (source(col) ^ at), held, result)
+    return result
+
+
+def fast_local(front_block, child_tiles, child_rows, child_cols, child_owner):
+    front = front_block[0]
+    block_rows, block_cols = front.shape
+    row = lax.axis_index("row")
+    col = lax.axis_index("col")
+    slots = pack(child_tiles[0], child_rows[0], child_cols[0], child_owner[0], 16)
+    slots = lax.all_to_all(slots, GRID, split_axis=0, concat_axis=0, tiled=True)
+    rows = slots[:, CR + 1, :CR].astype(jnp.int32).reshape(1, -1)
+    high, low = expand(slots, block_cols)
+    assembled = assemble(front, rows, high, low)
+    holds = ((row == 0) & (col == 0)).astype(jnp.int32)
+    factor_rows, inverse = factor(assembled[:P_SIZE, :P_SIZE], holds)
+    strips = []
+    for c in range(0, P_SIZE, STRIP):
+        strip = inverse[c : c + STRIP, : c + STRIP]
+        strip = down_columns(strip, col, (0,))
+        one = lax.ppermute(strip, GRID, [(c, 4 + c) for c in range(4)])
+        two = lax.ppermute(strip, GRID, [(c, 8 + c) for c in range(4)])
+        three = lax.ppermute(one, GRID, [(4 + c, 12 + c) for c in range(4)])
+        strip = jnp.where(row == 0, strip, jnp.where(row == 1, one, jnp.where(row == 2, two, three)))
+        strips.append(strip)
+    size = block_rows // CHUNKS
+    row_chunks, col_chunks = [], []
+    for at in range(CHUNKS):
+        top = at * size
+        part = assembled[top : top + size, :P_SIZE]
+        top_rows = top < P_SIZE
+        part = down_columns(part, col, (1, 2, 3) if top_rows else (0, 1, 2, 3))
+        row_chunks.append(part)
+        half = size // 2
+        cols = (1, 2, 3) if top_rows else (0, 1, 2, 3)
+        source = lambda c: c
+        first = in_plane(part[:half], row, col, cols, source, (1, 2, 1))
+        second = in_plane(part[half:], row, col, cols, source, (2, 1, 2))
+        col_chunks += [first, second]
+    row_solved = solve(jnp.concatenate(row_chunks, 0), strips)
+    col_solved = solve(jnp.concatenate(col_chunks, 0), strips)
+    place = jnp.stack([row, col]).astype(jnp.int32)
+    return update(place, row_solved, col_solved, assembled, factor_rows)[None]
 
 
 def blocked_factor(symmetric):
@@ -120,6 +548,11 @@
         P("front", ("row", "col"), None),
         P("front", ("row", "col")),
     )
+    square = mesh.shape["row"] == 4 and mesh.shape["col"] == 4
     return jax.shard_map(
-        local, mesh=mesh, in_specs=placed, out_specs=P("front", "row", "col"), check_vma=False
+        fast_local if square else local,
+        mesh=mesh,
+        in_specs=placed,
+        out_specs=P("front", "row", "col"),
+        check_vma=False,
     )

time: 1560 us -> 765 us (0.49)
  other arithmetic: 645 us -> 42.6 us
  waiting for transfers between devices: 617 us -> 282 us
  starting transfers between devices: 19.9 us -> 321 us
  matrix products: 175 us -> 0 us
  Pallas kernels: 0 us -> 81.7 us
  local copies, waits for them, and re-layouts: 75.3 us -> 23.4 us
    psum x3 -> x0, waiting for transfers between devices: 606 us -> none  [spread(): return lax.psum(jnp.where(mine, array, jnp.zeros_like(array)), axis)]
    unnamed x12 -> x22, other arithmetic: 423 us -> 30 us
    ppermute x0 -> x96, starting transfers between devices: none -> 314 us  [the longest x48 145 us: in_plane(): held = lax.ppermute(held, GRID, pairs)]
    ppermute x0 -> x96, waiting for transfers between devices: none -> 271 us  [the longest x4 121 us: fast_local(): two = lax.ppermute(strip, GRID, [(c, 8 + c) for c in range(4)])]
    another operation x40 -> x1, other arithmetic: 190 us -> 0.56 us  [fast_local(): place = jnp.stack([row, col]).astype(jnp.int32)]
    dot_general x30 -> x0, matrix products: 172 us -> none  [the longest x1 63.5 us: local(): jnp.dot(lower_part, column_part.T, precision=lax.Precision.HIGHEST)]
    pallas_call x0 -> x7, Pallas kernels: none -> 81.7 us  [the longest x1 34.3 us: update(): pl.pallas_call(functools.partial(update_kernel, step), grid=(count // ste...]
    scatter-add x1 -> x0, local copies, waits for them, and re-layouts: 18 us -> none  [local(): front_part.at[recv_rows[:, :, None], recv_cols[:, None, :]].add(recv_tiles)]
  transfers between devices with their start and end apart: 6 -> 97, of which waited for: 5 -> 19; matrix products, arithmetic and copies ran while one was open for 1% -> 7% of each run, Pallas kernels for 0% -> 2%
where the time goes in v1:
time: 765 us; the launch traced here: 754 us
  starting transfers between devices  321 us (42%)
  waiting for transfers between devices  282 us (37%)
  Pallas kernels  81.7 us (11%)
  other arithmetic  42.6 us (6%)
  local copies, waits for them, and re-layouts  23.4 us (3%)
    ppermute x48, starting transfers between devices, in_plane(): held = lax.ppermute(held, GRID, pairs)  145 us
    ppermute x4, waiting for transfers between devices, fast_local(): two = lax.ppermute(strip, GRID, [(c, 8 + c) for c in range(4)])  121 us
    ppermute x12, starting transfers between devices, down_columns(): one = lax.ppermute(middle, GRID, moves[1])  107 us
    ppermute x12, waiting for transfers between devices, down_columns(): one = lax.ppermute(middle, GRID, moves[1])  105 us
    ppermute x48, waiting for transfers between devices, in_plane(): held = lax.ppermute(held, GRID, pairs)  44.6 us
    pallas_call x1, Pallas kernels, update(): pl.pallas_call(functools.partial(update_kernel, step), grid=(count // ste...  34.3 us
    unnamed x22, other arithmetic  30 us
    ppermute x12, starting transfers between devices, down_columns(): middle = lax.ppermute(part, GRID, moves[0])  23.8 us
  transfers between devices with their start and end apart: 97, of which 19 were waited for; matrix products, arithmetic and copies ran while one was open for 7% of the time, Pallas kernels for 2%

profile of v1, /device:TPU:12, one launch (start us, length us, event | category | flops | bytes accessed | tf_op | source)
XLA Modules:
  0.0 753.5 jit_solution(12764538628421921137)
XLA Ops:
  3.1 7.2 all-to-all-start
  10.3 10.6 %all-to-all-done.slots_ref = f32[32,24,128]{2,1,0:T(8,128)S(1)} async-done(((f32[32,24,128]{2,1,0:T(8,128)}), f32[32,24,128]{2,1,0:T(8,128)S(1)}, u32[]{:S(2)}, u32[]{:S(2)}) %all-to-all-start) | async-done | bytes 393248 | tf_op jit(solution)/shard_map/all_to_all | solution.py:411
  21.0 6.0 expand_columns.1
  27.1 17.1 %assemble.1.front_ref = f32[2048,2048]{1,0:T(8,128)} custom-call(s32[1,512]{1,0:T(1,128)S(1)} %convert_element_type.15.rows_ref, bf16[2048,512]{1,0:T(8,128)(2,1)S(1)} %get-tuple-element.13.high_ref, bf16[2048,512]{1,0:T(8,128)(2,1)S(1)} %get-tuple-element.14.low_ref, f32[2048,2048]{1,0:T(8,128)} %bitcast.11), custom_call_target="tpu_custom_call" | custom-call | tf_op jit(solution)/shard_map/assemble/pallas_call | solution.py:270
  65.3 97.5 %collective-permute-done.28 = f32[256,256]{1,0:T(8,128)S(1)} collective-permute-done((f32[256,256]{1,0:T(8,128)S(1)}, f32[256,256]{1,0:T(8,128)S(1)}, u32[]{:S(2)}, u32[]{:S(2)}) %collective-permute-start.28) | collective-permute-done | bytes 262176 | tf_op jit(solution)/shard_map/ppermute | solution.py:422
  171.8 33.7 %collective-permute-done.1 = f32[256,1024]{1,0:T(8,128)S(1)} collective-permute-done((f32[256,1024]{1,0:T(8,128)S(1)}, f32[256,1024]{1,0:T(8,128)S(1)}, u32[]{:S(2)}, u32[]{:S(2)}) %collective-permute-start.1) | collective-permute-done | bytes 1048608 | tf_op jit(solution)/shard_map/ppermute | solution.py:388
  206.8 5.9 collective-permute-start.39
  212.7 6.7 constant_dynamic-update-slice_fusion.7
  227.3 18.2 %collective-permute-done.40 = f32[256,768]{1,0:T(8,128)S(1)} collective-permute-done((f32[256,768]{1,0:T(8,128)S(1)}, f32[256,768]{1,0:T(8,128)S(1)}, u32[]{:S(2)}, u32[]{:S(2)}) %collective-permute-start.40) | collective-permute-done | bytes 786464 | tf_op jit(solution)/shard_map/ppermute | solution.py:422
  247.2 8.1 %collective-permute-done.49 = f32[128,1024]{1,0:T(8,128)S(1)} collective-permute-done((f32[128,1024]{1,0:T(8,128)S(1)}, f32[128,1024]{1,0:T(8,128)S(1)}, u32[]{:S(2)}, u32[]{:S(2)}) %collective-permute-start.49) | collective-permute-done | bytes 524320 | tf_op jit(solution)/shard_map/ppermute | solution.py:399
  256.9 3.8 collective-permute-done.52
  260.7 4.6 collective-permute-start.15
  265.3 7.4 collective-permute-start.18
  281.2 89.5 %collective-permute-start.7 = (f32[256,1024]{1,0:T(8,128)}, f32[256,1024]{1,0:T(8,128)S(1)}, u32[]{:S(2)}, u32[]{:S(2)}) collective-permute-start(f32[256,1024]{1,0:T(8,128)} %copy-done.17), channel_id=1, source_target_pairs={{6,5},{10,9},{14,13},{22,21},{26,25},{30,29}} | collective-permute-start | bytes 3145736 | tf_op jit(solution)/shard_map/ppermute | solution.py:388
  370.7 6.5 collective-permute-start.8
  380.3 6.5 collective-permute-start.10
  388.3 7.7 %collective-permute-start.11 = (f32[256,1024]{1,0:T(8,128)}, f32[256,1024]{1,0:T(8,128)S(1)}, u32[]{:S(2)}, u32[]{:S(2)}) collective-permute-start(f32[256,1024]{1,0:T(8,128)} %collective-permute-done.9), channel_id=1, source_target_pairs={{6,7},{10,11},{14,15},{22,23},{26,27},{30,31}} | collective-permute-start | bytes 3145736 | tf_op jit(solution)/shard_map/ppermute | solution.py:389
  402.3 17.1 %collective-permute-done.10 = f32[256,1024]{1,0:T(8,128)S(1)} collective-permute-done((f32[256,1024]{1,0:T(8,128)}, f32[256,1024]{1,0:T(8,128)S(1)}, u32[]{:S(2)}, u32[]{:S(2)}) %collective-permute-start.10) | collective-permute-done | bytes 1048608 | tf_op jit(solution)/shard_map/ppermute | solution.py:388
  423.6 18.3 %collective-permute-done.13 = f32[256,1024]{1,0:T(8,128)S(1)} collective-permute-done((f32[256,1024]{1,0:T(8,128)}, f32[256,1024]{1,0:T(8,128)S(1)}, u32[]{:S(2)}, u32[]{:S(2)}) %collective-permute-start.13) | collective-permute-done | bytes 1048608 | tf_op jit(solution)/shard_map/ppermute | solution.py:388
  443.9 20.4 %collective-permute-done.16 = f32[256,1024]{1,0:T(8,128)S(1)} collective-permute-done((f32[256,1024]{1,0:T(8,128)}, f32[256,1024]{1,0:T(8,128)S(1)}, u32[]{:S(2)}, u32[]{:S(2)}) %collective-permute-start.16) | collective-permute-done | bytes 1048608 | tf_op jit(solution)/shard_map/ppermute | solution.py:388
  476.0 4.6 collective-permute-start.53
  480.7 6.1 collective-permute-done.19
  491.0 5.7 collective-permute-done.46
  499.0 9.7 %collective-permute-done.22 = f32[256,1024]{1,0:T(8,128)S(1)} collective-permute-done((f32[256,1024]{1,0:T(8,128)S(1)}, f32[256,1024]{1,0:T(8,128)S(1)}, u32[]{:S(2)}, u32[]{:S(2)}) %collective-permute-start.22) | collective-permute-done | bytes 1048608 | tf_op jit(solution)/shard_map/ppermute | solution.py:388
  508.8 6.2 collective-permute-start.60
  515.1 7.8 %collective-permute-start.63 = (f32[128,1024]{1,0:T(8,128)S(1)}, f32[128,1024]{1,0:T(8,128)}, u32[]{:S(2)}, u32[]{:S(2)}) collective-permute-start(f32[128,1024]{1,0:T(8,128)S(1)} %get-tuple-element.54), channel_id=1, source_target_pairs={{5,13},{10,2},{15,7},{21,29},{26,18},{31,23}} | collective-permute-start | bytes 1572872 | tf_op jit(solution)/shard_map/ppermute | solution.py:399
  522.9 7.0 collective-permute-start.66
  530.0 7.0 collective-permute-start.69
  539.5 8.8 %collective-permute-start.78 = (f32[128,1024]{1,0:T(8,128)S(1)}, f32[128,1024]{1,0:T(8,128)S(1)}, u32[]{:S(2)}, u32[]{:S(2)}) collective-permute-start(f32[128,1024]{1,0:T(8,128)S(1)} %get-tuple-element.49), channel_id=1, source_target_pairs={{0,4},{5,1},{10,14},{15,11},{16,20},{21,17},{26,30},{31,27}} | collective-permute-start | bytes 1572872 | tf_op jit(solution)/shard_map/ppermute | solution.py:399
  549.1 7.0 collective-permute-start.81
  556.9 7.2 collective-permute-start.84
  574.2 6.7 collective-permute-done.55
  583.5 11.3 %solve_rows.2 = (bf16[2048,1024]{1,0:T(8,128)(2,1)S(1)}, bf16[2048,1024]{1,0:T(8,128)(2,1)S(1)}) custom-call(f32[2048,1024]{1,0:T(8,128)} %get-tuple-element.21.rows_ref, f32[256,256]{1,0:T(8,128)S(1)} %select_select_fusion.14.refs_0_, f32[256,512]{1,0:T(8,128)S(1)} %select_select_fusion.12.refs_1_, f32[256,768]{1,0:T(8,128)S(1)} %select_select_fusion.10.refs_2_, ...), custom_call_target="tpu_custom_call" | custom-call | tf_op jit(solution)/shard_map/solve_rows/pallas_call | solution.py:307
  603.1 4.6 collective-permute-start.62
  617.6 4.6 collective-permute-start.68
  631.1 4.0 collective-permute-start.74
  638.8 4.8 collective-permute-done.79
  646.2 8.6 %collective-permute-done.85 = f32[128,1024]{1,0:T(8,128)S(1)} collective-permute-done((f32[128,1024]{1,0:T(8,128)S(1)}, f32[128,1024]{1,0:T(8,128)S(1)}, u32[]{:S(2)}, u32[]{:S(2)}) %collective-permute-start.85) | collective-permute-done | bytes 524320 | tf_op jit(solution)/shard_map/ppermute | solution.py:399
  656.2 4.6 collective-permute-start.80
  662.5 6.7 collective-permute-start.86
  669.2 6.4 collective-permute-start.89
  675.6 6.4 collective-permute-start.92
  682.0 6.7 collective-permute-start.95
  689.4 4.4 collective-permute-done.92
  693.9 6.3 collective-permute-done.95
  700.3 3.4 copy-done.6
  703.7 11.2 %solve_rows.3 = (bf16[2048,1024]{1,0:T(8,128)(2,1)S(1)}, bf16[2048,1024]{1,0:T(8,128)(2,1)S(1)}) custom-call(f32[2048,1024]{1,0:T(8,128)} %copy-done.6, f32[256,256]{1,0:T(8,128)S(1)} %select_select_fusion.14.refs_0_, f32[256,512]{1,0:T(8,128)S(1)} %select_select_fusion.12.refs_1_, f32[256,768]{1,0:T(8,128)S(1)} %select_select_fusion.10.refs_2_, ...), custom_call_target="tpu_custom_call" | custom-call | tf_op jit(solution)/shard_map/solve_rows/pallas_call | solution.py:307
  718.8 34.3 %schur_update.1 = f32[2048,2048]{1,0:T(8,128)} custom-call(s32[2]{0:T(128)} %pad_add_fusion.place_ref, bf16[2048,1024]{1,0:T(8,128)(2,1)} %copy-done.2, bf16[2048,1024]{1,0:T(8,128)(2,1)} %copy-done.3, bf16[2048,1024]{1,0:T(8,128)(2,1)} %copy-done.4, bf16[2048,1024]{1,0:T(8,128)(2,1)} %copy-done.5, f32[2048,2048]{1,0:T(8,128)} %assemble.1.front_ref, ...), custom_call_target="tpu_custom_call" | custom-call | tf_op jit(solution)/shard_map/schur_update/pallas_call | solution.py:356
  (307 shorter events, 146.2 us)
Async XLA Ops:
  53.7 109.7 %collective-permute-start = (f32[256,1024]{1,0:T(8,128)S(1)}, f32[256,1024]{1,0:T(8,128)S(1)}, u32[]{:S(2)}, u32[]{:S(2)}) collective-permute-start(f32[256,1024]{1,0:T(8,128)S(1)} %slice.121), channel_id=1, source_target_pairs={{4,6},{8,10},{12,14},{20,22},{24,26},{28,30}} | collective-permute-start | bytes 3145736 | tf_op jit(solution)/shard_map/ppermute | solution.py:387
  60.5 103.7 %collective-permute-start.31 = (f32[256,512]{1,0:T(8,128)}, f32[256,512]{1,0:T(8,128)S(1)}, u32[]{:S(2)}, u32[]{:S(2)}) collective-permute-start(f32[256,512]{1,0:T(8,128)} %collective-permute-done.30), channel_id=1, source_target_pairs={{2,1},{18,17}} | collective-permute-start | bytes 1572872 | tf_op jit(solution)/shard_map/ppermute | solution.py:388
  61.2 104.3 %collective-permute-start.32 = (f32[256,512]{1,0:T(8,128)}, f32[256,512]{1,0:T(8,128)S(1)}, u32[]{:S(2)}, u32[]{:S(2)}) collective-permute-start(f32[256,512]{1,0:T(8,128)} %collective-permute-done.30), channel_id=1, source_target_pairs={{2,3},{18,19}} | collective-permute-start | bytes 1572872 | tf_op jit(solution)/shard_map/ppermute | solution.py:389
  63.2 104.3 %collective-permute-start.42 = (f32[256,1024]{1,0:T(8,128)S(1)}, f32[256,1024]{1,0:T(8,128)S(1)}, u32[]{:S(2)}, u32[]{:S(2)}) collective-permute-start(f32[256,1024]{1,0:T(8,128)S(1)} %slice.103), channel_id=1, source_target_pairs={{0,2},{16,18}} | collective-permute-start | bytes 3145736 | tf_op jit(solution)/shard_map/ppermute | solution.py:387
  64.0 98.8 %collective-permute-start.28 = (f32[256,256]{1,0:T(8,128)S(1)}, f32[256,256]{1,0:T(8,128)S(1)}, u32[]{:S(2)}, u32[]{:S(2)}) collective-permute-start(f32[256,256]{1,0:T(8,128)S(1)} %select_select_fusion.15), channel_id=1, source_target_pairs={{0,8},{1,9},{2,10},{3,11},{16,24},{17,25},{18,26},{19,27}} | collective-permute-start | bytes 786440 | tf_op jit(solution)/shard_map/ppermute | solution.py:422
  164.2 41.3 %collective-permute-start.1 = (f32[256,1024]{1,0:T(8,128)S(1)}, f32[256,1024]{1,0:T(8,128)S(1)}, u32[]{:S(2)}, u32[]{:S(2)}) collective-permute-start(f32[256,1024]{1,0:T(8,128)S(1)} %collective-permute-done), channel_id=1, source_target_pairs={{6,5},{10,9},{14,13},{22,21},{26,25},{30,29}} | collective-permute-start | bytes 3145736 | tf_op jit(solution)/shard_map/ppermute | solution.py:388
  165.5 41.2 %collective-permute-start.2 = (f32[256,1024]{1,0:T(8,128)S(1)}, f32[256,1024]{1,0:T(8,128)S(1)}, u32[]{:S(2)}, u32[]{:S(2)}) collective-permute-start(f32[256,1024]{1,0:T(8,128)S(1)} %collective-permute-done), channel_id=1, source_target_pairs={{6,7},{10,11},{14,15},{22,23},{26,27},{30,31}} | collective-permute-start | bytes 3145736 | tf_op jit(solution)/shard_map/ppermute | solution.py:389
  168.3 52.7 %collective-permute-start.43 = (f32[256,1024]{1,0:T(8,128)S(1)}, f32[256,1024]{1,0:T(8,128)S(1)}, u32[]{:S(2)}, u32[]{:S(2)}) collective-permute-start(f32[256,1024]{1,0:T(8,128)S(1)} %collective-permute-done.42), channel_id=1, source_target_pairs={{2,1},{18,17}} | collective-permute-start | bytes 3145736 | tf_op jit(solution)/shard_map/ppermute | solution.py:388
  169.0 52.8 %collective-permute-start.44 = (f32[256,1024]{1,0:T(8,128)S(1)}, f32[256,1024]{1,0:T(8,128)S(1)}, u32[]{:S(2)}, u32[]{:S(2)}) collective-permute-start(f32[256,1024]{1,0:T(8,128)S(1)} %collective-permute-done.42), channel_id=1, source_target_pairs={{2,3},{18,19}} | collective-permute-start | bytes 3145736 | tf_op jit(solution)/shard_map/ppermute | solution.py:389
  171.1 48.3 %collective-permute-start.33 = (f32[256,512]{1,0:T(8,128)S(1)}, f32[256,512]{1,0:T(8,128)S(1)}, u32[]{:S(2)}, u32[]{:S(2)}) collective-permute-start(f32[256,512]{1,0:T(8,128)S(1)} %select_select_fusion.13), channel_id=1, source_target_pairs={{0,4},{1,5},{2,6},{3,7},{16,20},{17,21},{18,22},{19,23}} | collective-permute-start | bytes 1572872 | tf_op jit(solution)/shard_map/ppermute | solution.py:421
  221.8 43.5 %collective-permute-start.3 = (f32[256,1024]{1,0:T(8,128)S(1)}, f32[256,1024]{1,0:T(8,128)S(1)}, u32[]{:S(2)}, u32[]{:S(2)}) collective-permute-start(f32[256,1024]{1,0:T(8,128)S(1)} %get-tuple-element.43), channel_id=1, source_target_pairs={{4,6},{8,10},{12,14},{20,22},{24,26},{28,30}} | collective-permute-start | bytes 3145736 | tf_op jit(solution)/shard_map/ppermute | solution.py:387
  223.9 48.8 %collective-permute-start.6 = (f32[256,1024]{1,0:T(8,128)S(1)}, f32[256,1024]{1,0:T(8,128)S(1)}, u32[]{:S(2)}, u32[]{:S(2)}) collective-permute-start(f32[256,1024]{1,0:T(8,128)S(1)} %get-tuple-element.42), channel_id=1, source_target_pairs={{4,6},{8,10},{12,14},{20,22},{24,26},{28,30}} | collective-permute-start | bytes 3145736 | tf_op jit(solution)/shard_map/ppermute | solution.py:387
  224.6 30.6 %collective-permute-start.49 = (f32[128,1024]{1,0:T(8,128)S(1)}, f32[128,1024]{1,0:T(8,128)S(1)}, u32[]{:S(2)}, u32[]{:S(2)}) collective-permute-start(f32[128,1024]{1,0:T(8,128)S(1)} %collective-permute-done.48), channel_id=1, source_target_pairs={{1,9},{14,6},{11,3},{17,25},{30,22},{27,19}} | collective-permute-start | bytes 1572872 | tf_op jit(solution)/shard_map/ppermute | solution.py:399
  226.0 34.7 %collective-permute-start.52 = (f32[128,1024]{1,0:T(8,128)S(1)}, f32[128,1024]{1,0:T(8,128)S(1)}, u32[]{:S(2)}, u32[]{:S(2)}) collective-permute-start(f32[128,1024]{1,0:T(8,128)S(1)} %collective-permute-done.51), channel_id=1, source_target_pairs={{13,9},{2,6},{7,3},{29,25},{18,22},{23,19}} | collective-permute-start | bytes 1572872 | tf_op jit(solution)/shard_map/ppermute | solution.py:399
  245.5 30.3 %collective-permute-start.9 = (f32[256,1024]{1,0:T(8,128)}, f32[256,1024]{1,0:T(8,128)}, u32[]{:S(2)}, u32[]{:S(2)}) collective-permute-start(f32[256,1024]{1,0:T(8,128)} %get-tuple-element.41), channel_id=1, source_target_pairs={{4,6},{8,10},{12,14},{20,22},{24,26},{28,30}} | collective-permute-start | bytes 3145736 | tf_op jit(solution)/shard_map/ppermute | solution.py:387
  273.7 97.0 %collective-permute-start.41 = (f32[256,768]{1,0:T(8,128)}, f32[256,768]{1,0:T(8,128)}, u32[]{:S(2)}, u32[]{:S(2)}) collective-permute-start(f32[256,768]{1,0:T(8,128)} %collective-permute-done.39), channel_id=1, source_target_pairs={{4,12},{5,13},{6,14},{7,15},{20,28},{21,29},{22,30},{23,31}} | collective-permute-start | bytes 2359304 | tf_op jit(solution)/shard_map/ppermute | solution.py:423
  275.8 104.5 %collective-permute-start.50 = (f32[128,1024]{1,0:T(8,128)}, f32[128,1024]{1,0:T(8,128)S(1)}, u32[]{:S(2)}, u32[]{:S(2)}) collective-permute-start(f32[128,1024]{1,0:T(8,128)} %copy-done.46), channel_id=1, source_target_pairs={{9,13},{6,2},{3,7},{25,29},{22,18},{19,23}} | collective-permute-start | bytes 1572872 | tf_op jit(solution)/shard_map/ppermute | solution.py:399
  279.1 109.2 %collective-permute-start.4 = (f32[256,1024]{1,0:T(8,128)}, f32[256,1024]{1,0:T(8,128)S(1)}, u32[]{:S(2)}, u32[]{:S(2)}) collective-permute-start(f32[256,1024]{1,0:T(8,128)} %copy-done.15), channel_id=1, source_target_pairs={{6,5},{10,9},{14,13},{22,21},{26,25},{30,29}} | collective-permute-start | bytes 3145736 | tf_op jit(solution)/shard_map/ppermute | solution.py:388
  280.4 115.5 %collective-permute-start.5 = (f32[256,1024]{1,0:T(8,128)}, f32[256,1024]{1,0:T(8,128)S(1)}, u32[]{:S(2)}, u32[]{:S(2)}) collective-permute-start(f32[256,1024]{1,0:T(8,128)} %copy-done.15), channel_id=1, source_target_pairs={{6,7},{10,11},{14,15},{22,23},{26,27},{30,31}} | collective-permute-start | bytes 3145736 | tf_op jit(solution)/shard_map/ppermute | solution.py:389
  281.2 116.1 %collective-permute-start.7 = (f32[256,1024]{1,0:T(8,128)}, f32[256,1024]{1,0:T(8,128)S(1)}, u32[]{:S(2)}, u32[]{:S(2)}) collective-permute-start(f32[256,1024]{1,0:T(8,128)} %copy-done.17), channel_id=1, source_target_pairs={{6,5},{10,9},{14,13},{22,21},{26,25},{30,29}} | collective-permute-start | bytes 3145736 | tf_op jit(solution)/shard_map/ppermute | solution.py:388
  370.7 27.3 %collective-permute-start.8 = (f32[256,1024]{1,0:T(8,128)}, f32[256,1024]{1,0:T(8,128)S(1)}, u32[]{:S(2)}, u32[]{:S(2)}) collective-permute-start(f32[256,1024]{1,0:T(8,128)} %copy-done.17), channel_id=1, source_target_pairs={{6,7},{10,11},{14,15},{22,23},{26,27},{30,31}} | collective-permute-start | bytes 3145736 | tf_op jit(solution)/shard_map/ppermute | solution.py:389
  380.3 39.1 %collective-permute-start.10 = (f32[256,1024]{1,0:T(8,128)}, f32[256,1024]{1,0:T(8,128)S(1)}, u32[]{:S(2)}, u32[]{:S(2)}) collective-permute-start(f32[256,1024]{1,0:T(8,128)} %collective-permute-done.9), channel_id=1, source_target_pairs={{6,5},{10,9},{14,13},{22,21},{26,25},{30,29}} | collective-permute-start | bytes 3145736 | tf_op jit(solution)/shard_map/ppermute | solution.py:388
  388.3 34.5 %collective-permute-start.11 = (f32[256,1024]{1,0:T(8,128)}, f32[256,1024]{1,0:T(8,128)S(1)}, u32[]{:S(2)}, u32[]{:S(2)}) collective-permute-start(f32[256,1024]{1,0:T(8,128)} %collective-permute-done.9), channel_id=1, source_target_pairs={{6,7},{10,11},{14,15},{22,23},{26,27},{30,31}} | collective-permute-start | bytes 3145736 | tf_op jit(solution)/shard_map/ppermute | solution.py:389
  395.9 45.9 %collective-permute-start.13 = (f32[256,1024]{1,0:T(8,128)}, f32[256,1024]{1,0:T(8,128)S(1)}, u32[]{:S(2)}, u32[]{:S(2)}) collective-permute-start(f32[256,1024]{1,0:T(8,128)} %collective-permute-done.12), channel_id=1, source_target_pairs={{2,1},{6,5},{10,9},{14,13},{18,17},{22,21},{26,25},{30,29}} | collective-permute-start | bytes 3145736 | tf_op jit(solution)/shard_map/ppermute | solution.py:388
  397.3 45.3 %collective-permute-start.14 = (f32[256,1024]{1,0:T(8,128)}, f32[256,1024]{1,0:T(8,128)S(1)}, u32[]{:S(2)}, u32[]{:S(2)}) collective-permute-start(f32[256,1024]{1,0:T(8,128)} %collective-permute-done.12), channel_id=1, source_target_pairs={{2,3},{6,7},{10,11},{14,15},{18,19},{22,23},{26,27},{30,31}} | collective-permute-start | bytes 3145736 | tf_op jit(solution)/shard_map/ppermute | solution.py:389
  398.0 66.3 %collective-permute-start.16 = (f32[256,1024]{1,0:T(8,128)}, f32[256,1024]{1,0:T(8,128)S(1)}, u32[]{:S(2)}, u32[]{:S(2)}) collective-permute-start(f32[256,1024]{1,0:T(8,128)} %collective-permute-done.15), channel_id=1, source_target_pairs={{2,1},{6,5},{10,9},{14,13},{18,17},{22,21},{26,25},{30,29}} | collective-permute-start | bytes 3145736 | tf_op jit(solution)/shard_map/ppermute | solution.py:388
  419.4 51.2 %collective-permute-start.17 = (f32[256,1024]{1,0:T(8,128)}, f32[256,1024]{1,0:T(8,128)S(1)}, u32[]{:S(2)}, u32[]{:S(2)}) collective-permute-start(f32[256,1024]{1,0:T(8,128)} %collective-permute-done.15), channel_id=1, source_target_pairs={{2,3},{6,7},{10,11},{14,15},{18,19},{22,23},{26,27},{30,31}} | collective-permute-start | bytes 3145736 | tf_op jit(solution)/shard_map/ppermute | solution.py:389
  422.8 51.8 %collective-permute-start.21 = (f32[256,1024]{1,0:T(8,128)S(1)}, f32[256,1024]{1,0:T(8,128)S(1)}, u32[]{:S(2)}, u32[]{:S(2)}) collective-permute-start(f32[256,1024]{1,0:T(8,128)S(1)} %get-tuple-element.37), channel_id=1, source_target_pairs={{0,2},{4,6},{8,10},{12,14},{16,18},{20,22},{24,26},{28,30}} | collective-permute-start | bytes 3145736 | tf_op jit(solution)/shard_map/ppermute | solution.py:387
  441.9 34.2 %collective-permute-start.45 = (f32[256,1024]{1,0:T(8,128)S(1)}, f32[256,1024]{1,0:T(8,128)S(1)}, u32[]{:S(2)}, u32[]{:S(2)}) collective-permute-start(f32[256,1024]{1,0:T(8,128)S(1)} %select_select_fusion.1), channel_id=1, source_target_pairs={{0,4},{1,5},{2,6},{3,7},{16,20},{17,21},{18,22},{19,23}} | collective-permute-start | bytes 3145736 | tf_op jit(solution)/shard_map/ppermute | solution.py:421
  442.6 44.2 %collective-permute-start.19 = (f32[256,1024]{1,0:T(8,128)}, f32[256,1024]{1,0:T(8,128)S(1)}, u32[]{:S(2)}, u32[]{:S(2)}) collective-permute-start(f32[256,1024]{1,0:T(8,128)} %collective-permute-done.18), channel_id=1, source_target_pairs={{2,1},{6,5},{10,9},{14,13},{18,17},{22,21},{26,25},{30,29}} | collective-permute-start | bytes 3145736 | tf_op jit(solution)/shard_map/ppermute | solution.py:388
  470.6 26.1 %collective-permute-start.46 = (f32[256,1024]{1,0:T(8,128)S(1)}, f32[256,1024]{1,0:T(8,128)S(1)}, u32[]{:S(2)}, u32[]{:S(2)}) collective-permute-start(f32[256,1024]{1,0:T(8,128)S(1)} %select_select_fusion.1), channel_id=1, source_target_pairs={{0,8},{1,9},{2,10},{3,11},{16,24},{17,25},{18,26},{19,27}} | collective-permute-start | bytes 3145736 | tf_op jit(solution)/shard_map/ppermute | solution.py:422
  474.6 34.2 %collective-permute-start.22 = (f32[256,1024]{1,0:T(8,128)S(1)}, f32[256,1024]{1,0:T(8,128)S(1)}, u32[]{:S(2)}, u32[]{:S(2)}) collective-permute-start(f32[256,1024]{1,0:T(8,128)S(1)} %collective-permute-done.21), channel_id=1, source_target_pairs={{2,1},{6,5},{10,9},{14,13},{18,17},{22,21},{26,25},{30,29}} | collective-permute-start | bytes 3145736 | tf_op jit(solution)/shard_map/ppermute | solution.py:388
  486.8 28.3 %collective-permute-start.23 = (f32[256,1024]{1,0:T(8,128)S(1)}, f32[256,1024]{1,0:T(8,128)S(1)}, u32[]{:S(2)}, u32[]{:S(2)}) collective-permute-start(f32[256,1024]{1,0:T(8,128)S(1)} %collective-permute-done.21), channel_id=1, source_target_pairs={{2,3},{6,7},{10,11},{14,15},{18,19},{22,23},{26,27},{30,31}} | collective-permute-start | bytes 3145736 | tf_op jit(solution)/shard_map/ppermute | solution.py:389
  487.5 35.4 %collective-permute-start.47 = (f32[256,1024]{1,0:T(8,128)S(1)}, f32[256,1024]{1,0:T(8,128)S(1)}, u32[]{:S(2)}, u32[]{:S(2)}) collective-permute-start(f32[256,1024]{1,0:T(8,128)S(1)} %collective-permute-done.45), channel_id=1, source_target_pairs={{4,12},{5,13},{6,14},{7,15},{20,28},{21,29},{22,30},{23,31}} | collective-permute-start | bytes 3145736 | tf_op jit(solution)/shard_map/ppermute | solution.py:423
  496.7 33.2 %collective-permute-start.54 = (f32[128,1024]{1,0:T(8,128)S(1)}, f32[128,1024]{1,0:T(8,128)S(1)}, u32[]{:S(2)}, u32[]{:S(2)}) collective-permute-start(f32[128,1024]{1,0:T(8,128)S(1)} %get-tuple-element.57), channel_id=1, source_target_pairs={{5,1},{10,14},{15,11},{21,17},{26,30},{31,27}} | collective-permute-start | bytes 1572872 | tf_op jit(solution)/shard_map/ppermute | solution.py:399
  497.4 39.6 %collective-permute-start.57 = (f32[128,1024]{1,0:T(8,128)S(1)}, f32[128,1024]{1,0:T(8,128)}, u32[]{:S(2)}, u32[]{:S(2)}) collective-permute-start(f32[128,1024]{1,0:T(8,128)S(1)} %get-tuple-element.56), channel_id=1, source_target_pairs={{5,13},{10,2},{15,7},{21,29},{26,18},{31,23}} | collective-permute-start | bytes 1572872 | tf_op jit(solution)/shard_map/ppermute | solution.py:399
  508.8 29.0 %collective-permute-start.60 = (f32[128,1024]{1,0:T(8,128)S(1)}, f32[128,1024]{1,0:T(8,128)}, u32[]{:S(2)}, u32[]{:S(2)}) collective-permute-start(f32[128,1024]{1,0:T(8,128)S(1)} %get-tuple-element.55), channel_id=1, source_target_pairs={{5,1},{10,14},{15,11},{21,17},{26,30},{31,27}} | collective-permute-start | bytes 1572872 | tf_op jit(solution)/shard_map/ppermute | solution.py:399
  530.0 26.1 %collective-permute-start.69 = (f32[128,1024]{1,0:T(8,128)S(1)}, f32[128,1024]{1,0:T(8,128)S(1)}, u32[]{:S(2)}, u32[]{:S(2)}) collective-permute-start(f32[128,1024]{1,0:T(8,128)S(1)} %get-tuple-element.52), channel_id=1, source_target_pairs={{5,13},{10,2},{15,7},{21,29},{26,18},{31,23}} | collective-permute-start | bytes 1572872 | tf_op jit(solution)/shard_map/ppermute | solution.py:399
  537.0 27.1 %collective-permute-start.72 = (f32[128,1024]{1,0:T(8,128)S(1)}, f32[128,1024]{1,0:T(8,128)S(1)}, u32[]{:S(2)}, u32[]{:S(2)}) collective-permute-start(f32[128,1024]{1,0:T(8,128)S(1)} %get-tuple-element.51), channel_id=1, source_target_pairs={{0,4},{5,1},{10,14},{15,11},{16,20},{21,17},{26,30},{31,27}} | collective-permute-start | bytes 1572872 | tf_op jit(solution)/shard_map/ppermute | solution.py:399
  537.8 27.8 %collective-permute-start.75 = (f32[128,1024]{1,0:T(8,128)S(1)}, f32[128,1024]{1,0:T(8,128)S(1)}, u32[]{:S(2)}, u32[]{:S(2)}) collective-permute-start(f32[128,1024]{1,0:T(8,128)S(1)} %get-tuple-element.50), channel_id=1, source_target_pairs={{0,8},{5,13},{10,2},{15,7},{16,24},{21,29},{26,18},{31,23}} | collective-permute-start | bytes 1572872 | tf_op jit(solution)/shard_map/ppermute | solution.py:399
  539.5 30.7 %collective-permute-start.78 = (f32[128,1024]{1,0:T(8,128)S(1)}, f32[128,1024]{1,0:T(8,128)S(1)}, u32[]{:S(2)}, u32[]{:S(2)}) collective-permute-start(f32[128,1024]{1,0:T(8,128)S(1)} %get-tuple-element.49), channel_id=1, source_target_pairs={{0,4},{5,1},{10,14},{15,11},{16,20},{21,17},{26,30},{31,27}} | collective-permute-start | bytes 1572872 | tf_op jit(solution)/shard_map/ppermute | solution.py:399
  565.7 29.2 %collective-permute-start.58 = (f32[128,1024]{1,0:T(8,128)}, f32[128,1024]{1,0:T(8,128)}, u32[]{:S(2)}, u32[]{:S(2)}) collective-permute-start(f32[128,1024]{1,0:T(8,128)} %collective-permute-done.57), channel_id=1, source_target_pairs={{13,9},{2,6},{7,3},{29,25},{18,22},{23,19}} | collective-permute-start | bytes 1572872 | tf_op jit(solution)/shard_map/ppermute | solution.py:399
  570.1 29.5 %collective-permute-start.87 = (f32[128,1024]{1,0:T(8,128)}, f32[128,1024]{1,0:T(8,128)}, u32[]{:S(2)}, u32[]{:S(2)}) collective-permute-start(f32[128,1024]{1,0:T(8,128)} %get-tuple-element.46), channel_id=1, source_target_pairs={{0,8},{5,13},{10,2},{15,7},{16,24},{21,29},{26,18},{31,23}} | collective-permute-start | bytes 1572872 | tf_op jit(solution)/shard_map/ppermute | solution.py:399
  571.6 28.9 %collective-permute-start.61 = (f32[128,1024]{1,0:T(8,128)}, f32[128,1024]{1,0:T(8,128)}, u32[]{:S(2)}, u32[]{:S(2)}) collective-permute-start(f32[128,1024]{1,0:T(8,128)} %collective-permute-done.60), channel_id=1, source_target_pairs={{1,9},{14,6},{11,3},{17,25},{30,22},{27,19}} | collective-permute-start | bytes 1572872 | tf_op jit(solution)/shard_map/ppermute | solution.py:399
  572.9 28.9 %collective-permute-start.64 = (f32[128,1024]{1,0:T(8,128)}, f32[128,1024]{1,0:T(8,128)}, u32[]{:S(2)}, u32[]{:S(2)}) collective-permute-start(f32[128,1024]{1,0:T(8,128)} %collective-permute-done.63), channel_id=1, source_target_pairs={{13,9},{2,6},{7,3},{29,25},{18,22},{23,19}} | collective-permute-start | bytes 1572872 | tf_op jit(solution)/shard_map/ppermute | solution.py:399
  656.2 25.9 %collective-permute-start.80 = (f32[128,1024]{1,0:T(8,128)S(1)}, f32[128,1024]{1,0:T(8,128)S(1)}, u32[]{:S(2)}, u32[]{:S(2)}) collective-permute-start(f32[128,1024]{1,0:T(8,128)S(1)} %collective-permute-done.79), channel_id=1, source_target_pairs={{12,8},{9,13},{6,2},{3,7},{28,24},{25,29},{22,18},{19,23}} | collective-permute-start | bytes 1572872 | tf_op jit(solution)/shard_map/ppermute | solution.py:399
  660.9 27.9 %collective-permute-start.83 = (f32[128,1024]{1,0:T(8,128)S(1)}, f32[128,1024]{1,0:T(8,128)S(1)}, u32[]{:S(2)}, u32[]{:S(2)}) collective-permute-start(f32[128,1024]{1,0:T(8,128)S(1)} %collective-permute-done.82), channel_id=1, source_target_pairs={{12,4},{9,1},{6,14},{3,11},{28,20},{25,17},{22,30},{19,27}} | collective-permute-start | bytes 1572872 | tf_op jit(solution)/shard_map/ppermute | solution.py:399
  662.5 26.5 %collective-permute-start.86 = (f32[128,1024]{1,0:T(8,128)S(1)}, f32[128,1024]{1,0:T(8,128)S(1)}, u32[]{:S(2)}, u32[]{:S(2)}) collective-permute-start(f32[128,1024]{1,0:T(8,128)S(1)} %collective-permute-done.85), channel_id=1, source_target_pairs={{12,8},{9,13},{6,2},{3,7},{28,24},{25,29},{22,18},{19,23}} | collective-permute-start | bytes 1572872 | tf_op jit(solution)/shard_map/ppermute | solution.py:399
  (100 other events, 2854.4 us)

commit v2 on v1

--- a/solution.py
+++ b/solution.py
@@ -101,84 +101,126 @@
 TN = ((0,), (0,))
 
 
-def factor_kernel(blocks, a_ref, l_ref, z_ref, u_ref, d_ref):
+def factor_step(blocks, j, z_ref, l_ref, u_ref, d_ref, left):
     def block(i):
         return pl.ds(pl.multiple_of(i * DB, DB), DB)
 
+    now = block(j)
+    base = pl.multiple_of(j * DB, DB)
+    tiles = [
+        z_ref[pl.ds(pl.multiple_of(base + GROUP * i, GROUP), GROUP), now] for i in range(DB // GROUP)
+    ]
+    upper, inverse = factor_tile(tiles)
+    for i in range(DB // GROUP):
+        u_ref[GROUP * i : GROUP * i + GROUP, now] = upper[i]
+        d_ref[GROUP * i : GROUP * i + GROUP, :] = inverse[i]
+        z_ref[pl.ds(pl.multiple_of(base + GROUP * i, GROUP), GROUP), now] = inverse[i]
+    m = d_ref[...]
+    l_ref[now, left] = u_ref[:, now].T
+    for c in range(0, blocks * DB, WIDE):
+        u_ref[:, c : c + WIDE] = dot(m, z_ref[now, c : c + WIDE])
+    u_ref[:, now] = m
+    z_ref[now, :] = u_ref[...]
+
+    def trail(i, _):
+        below = block(i)
+        ui = u_ref[:, below]
+        l_ref[below, left] = ui.T
+        z_ref[below, now] = jnp.zeros((DB, DB), F32)
+        for c in range(0, blocks * DB, WIDE):
+            z_ref[below, c : c + WIDE] = z_ref[below, c : c + WIDE] - dot(
+                ui, u_ref[:, c : c + WIDE], TN
+            )
+        return 0
+
+    lax.fori_loop(j + 1, blocks, trail, 0)
+
+
+def copy(source, target, sem):
+    return pltpu.make_async_copy(source, target, sem)
+
+
+def first_block(front_ref, rows_ref, high_ref, low_ref, a_ref, z_ref, sem):
+    size = a_ref.shape[0]
+    load = copy(front_ref.at[pl.ds(0, size), pl.ds(0, size)], a_ref, sem)
+    load.start()
+    load.wait()
+
+    def add(i, _):
+        part = pl.ds(pl.multiple_of(i * STRIP, STRIP), STRIP)
+        place = lax.broadcasted_iota(jnp.int32, (STRIP, rows_ref.shape[1]), 0) + i * STRIP
+        onehot = jnp.where(place == rows_ref[...], 1.0, 0.0).astype(BF16)
+        a_ref[part, :] += mm(onehot, high_ref[...], NT) + mm(onehot, low_ref[...], NT)
+        return 0
+
+    lax.fori_loop(0, size // STRIP, add, 0)
+
     def symmetric(i, _):
         def one(j, _):
-            z_ref[block(i), block(j)] = 0.5 * (a_ref[block(i), block(j)] + a_ref[block(j), block(i)].T)
+            bi = pl.ds(pl.multiple_of(i * DB, DB), DB)
+            bj = pl.ds(pl.multiple_of(j * DB, DB), DB)
+            z_ref[bi, bj] = 0.5 * (a_ref[bi, bj] + a_ref[bj, bi].T)
             return 0
 
-        lax.fori_loop(0, blocks, one, 0)
+        lax.fori_loop(0, size // DB, one, 0)
         return 0
 
-    lax.fori_loop(0, blocks, symmetric, 0)
-
-    def step(j, _):
-        now = block(j)
-        base = pl.multiple_of(j * DB, DB)
-        tiles = [
-            z_ref[pl.ds(pl.multiple_of(base + GROUP * i, GROUP), GROUP), now]
-            for i in range(DB // GROUP)
-        ]
-        upper, inverse = factor_tile(tiles)
-        for i in range(DB // GROUP):
-            u_ref[GROUP * i : GROUP * i + GROUP, now] = upper[i]
-            d_ref[GROUP * i : GROUP * i + GROUP, :] = inverse[i]
-            z_ref[pl.ds(pl.multiple_of(base + GROUP * i, GROUP), GROUP), now] = inverse[i]
-        m = d_ref[...]
-        l_ref[now, now] = u_ref[:, now].T
-        for c in range(0, blocks * DB, WIDE):
-            u_ref[:, c : c + WIDE] = dot(m, z_ref[now, c : c + WIDE])
-        u_ref[:, now] = m
-        z_ref[now, :] = u_ref[...]
-
-        def trail(i, _):
-            below = block(i)
-            ui = u_ref[:, below]
-            l_ref[below, now] = ui.T
-            l_ref[now, below] = jnp.zeros((DB, DB), F32)
-            z_ref[below, now] = jnp.zeros((DB, DB), F32)
-            for c in range(0, blocks * DB, WIDE):
-                z_ref[below, c : c + WIDE] = z_ref[below, c : c + WIDE] - dot(
-                    ui, u_ref[:, c : c + WIDE], TN
-                )
-            return 0
-
-        lax.fori_loop(j + 1, blocks, trail, 0)
-        return 0
-
-    lax.fori_loop(0, blocks, step, 0)
-
-    def clean(i, _):
-        def one(j, _):
-            z_ref[block(i), block(j)] = jnp.zeros((DB, DB), F32)
-            return 0
-
-        lax.fori_loop(i + 1, blocks, one, 0)
-        return 0
-
-    lax.fori_loop(0, blocks, clean, 0)
-
-
-def maybe_factor_kernel(blocks, holds_ref, a_ref, *rest):
+    lax.fori_loop(0, size // DB, symmetric, 0)
+
+
+def factor_kernel(top, tall, holds_ref, token_ref, *refs):
+    if top == 0:
+        front_ref, rows_ref, high_ref, low_ref = refs[:4]
+        z_out, l_out, strip_ref, a_ref, z_ref, l_ref, u_ref, d_ref, sem = refs[4:]
+    else:
+        z_in, l_in, z_out, l_out, strip_ref, z_ref, l_ref, u_ref, d_ref, sem = refs
+    size = z_ref.shape[0]
+    below = pl.ds(top, size - top)
+
+    def moved(source, target):
+        one = copy(source, target, sem)
+        one.start()
+        one.wait()
+
     @pl.when(holds_ref[0] == 1)
     def _():
-        factor_kernel(blocks, a_ref, *rest)
-
-
-def factor(block, holds):
-    size = block.shape[0]
+        if top == 0:
+            first_block(front_ref, rows_ref, high_ref, low_ref, a_ref, z_ref, sem)
+        else:
+            moved(z_in.at[below, :], z_ref.at[below, :])
+            l_ref[0:top, :] = jnp.zeros((top, tall), F32)
+        for k in range(DB, tall, DB):
+            l_ref[top + k - DB : top + k, k:] = jnp.zeros((DB, tall - k), F32)
+        for k in range(0, tall, DB):
+            factor_step(size // DB, (top + k) // DB, z_ref, l_ref, u_ref, d_ref, slice(k, k + DB))
+        for k in range(DB, tall, DB):
+            z_ref[top + k - DB : top + k, top + k : top + tall] = jnp.zeros((DB, tall - k), F32)
+        moved(z_ref.at[pl.ds(top, tall), pl.ds(0, top + tall)], strip_ref)
+        moved(l_ref, l_out.at[:, pl.ds(top, tall)])
+        if top + tall < size:
+            rest = pl.ds(top + tall, size - top - tall)
+            moved(z_ref.at[rest, :], z_out.at[rest, :])
+
+
+def factor(top, tall, holds, token, state, size):
+    anywhere = pl.BlockSpec(memory_space=pl.ANY)
+    resident = pl.BlockSpec(memory_space=VMEM)
+    square = jax.ShapeDtypeStruct((size, size), F32)
+    specs = [anywhere] + [resident] * 3 if top == 0 else [anywhere] * 2
+    scratch = [VMEM((size, size), F32)] if top == 0 else []
+    scratch += [VMEM((size, size), F32), VMEM((size, tall), F32), VMEM((DB, size), F32)]
+    scratch += [VMEM((DB, DB), F32), pltpu.SemaphoreType.DMA]
     return pl.pallas_call(
-        functools.partial(maybe_factor_kernel, size // DB),
-        out_shape=[jax.ShapeDtypeStruct((size, size), F32)] * 2,
-        in_specs=[pl.BlockSpec(memory_space=pltpu.SMEM), pl.BlockSpec(memory_space=VMEM)],
-        out_specs=[pl.BlockSpec(memory_space=VMEM)] * 2,
-        scratch_shapes=[VMEM((DB, size), F32), VMEM((DB, DB), F32)],
-        compiler_params=pltpu.CompilerParams(vmem_limit_bytes=40 * MIB),
+        functools.partial(factor_kernel, top, tall),
+        out_shape=[square, square, jax.ShapeDtypeStruct((tall, top + tall), F32)],
+        in_specs=[pl.BlockSpec(memory_space=pltpu.SMEM), anywhere] + specs,
+        out_specs=[anywhere] * 3,
+        scratch_shapes=scratch,
+        input_output_aliases={} if top == 0 else {2: 0, 3: 1},
+        compiler_params=pltpu.CompilerParams(vmem_limit_bytes=58 * MIB),
+        cost_estimate=pl.CostEstimate(flops=10**10, bytes_accessed=2 * 10**7, transcendentals=0),
         name="panel_factor",
-    )(jnp.full((1,), holds, jnp.int32), block)
+    )(holds, token, *state)
 
 
 def pack_kernel(groups, owner_ref, tile_ref, row_ref, col_ref, out_ref, seen_ref):
@@ -221,7 +263,7 @@
     return lax.dot_general(a, b, (dims, ((), ())), preferred_element_type=F32)
 
 
-def expand_kernel(slots_ref, high_ref, low_ref):
+def expand_kernel(token_ref, slots_ref, high_ref, low_ref):
     cols = high_ref.shape[0]
     place = lax.broadcasted_iota(jnp.int32, (cols, 2 * CC), 0)
     row = lax.broadcasted_iota(jnp.int32, (CC, CC), 0) // CR
@@ -243,27 +285,27 @@
     low_ref[...] = low
 
 
-def expand(slots, cols):
+def expand(slots, cols, token):
     count = slots.shape[0]
     return pl.pallas_call(
         expand_kernel,
         grid=(count // 8,),
         out_shape=[jax.ShapeDtypeStruct((cols, count * CR), BF16)] * 2,
-        in_specs=[pl.BlockSpec((8, SLOT, CC), lambda g: (g, 0, 0))],
+        in_specs=[pl.BlockSpec(memory_space=pl.ANY), pl.BlockSpec((8, SLOT, CC), lambda g: (g, 0, 0))],
         out_specs=[pl.BlockSpec((cols, CC), lambda g: (0, g))] * 2,
-        compiler_params=pltpu.CompilerParams(vmem_limit_bytes=40 * MIB),
+        compiler_params=pltpu.CompilerParams(vmem_limit_bytes=58 * MIB),
         name="expand_columns",
-    )(slots)
-
-
-def assemble_kernel(step, rows_ref, high_ref, low_ref, front_ref, out_ref):
+    )(token, slots)
+
+
+def assemble_kernel(step, token_ref, rows_ref, high_ref, low_ref, front_ref, out_ref):
     first = pl.program_id(0) * step
     place = lax.broadcasted_iota(jnp.int32, (step, rows_ref.shape[1]), 0) + first
     onehot = jnp.where(place == rows_ref[...], 1.0, 0.0).astype(BF16)
     out_ref[...] = front_ref[...] + (mm(onehot, high_ref[...], NT) + mm(onehot, low_ref[...], NT))
 
 
-def assemble(front, rows, high, low):
+def assemble(front, rows, high, low, token):
     step = 256
     count, width = front.shape
     k = rows.shape[1]
@@ -272,53 +314,118 @@
         grid=(count // step,),
         out_shape=jax.ShapeDtypeStruct((count, width), F32),
         in_specs=[
+            pl.BlockSpec(memory_space=pl.ANY),
             pl.BlockSpec((1, k), lambda i: (0, 0)),
             pl.BlockSpec((width, k), lambda i: (0, 0)),
             pl.BlockSpec((width, k), lambda i: (0, 0)),
             pl.BlockSpec((step, width), lambda i: (i, 0)),
         ],
         out_specs=pl.BlockSpec((step, width), lambda i: (i, 0)),
-        compiler_params=pltpu.CompilerParams(vmem_limit_bytes=40 * MIB),
+        compiler_params=pltpu.CompilerParams(vmem_limit_bytes=58 * MIB),
         name="assemble",
-    )(rows, high, low, front)
-
-
-def solve_kernel(rows_ref, *refs):
-    strips = refs[: P_SIZE // STRIP]
-    out_high_ref, out_low_ref, high_ref, low_ref = refs[P_SIZE // STRIP :]
-
-    @pl.when(pl.program_id(0) == 0)
+    )(token, rows, high, low, front)
+
+
+def pick(cases, case_ref, at, target, sem):
+    for number, source in cases:
+
+        @pl.when(case_ref[at] == number)
+        def _(source=source):
+            copy(source, target, sem).start()
+
+
+def pick(cases, who_ref, target, sem):
+    for at, number, source in cases:
+
+        @pl.when(who_ref[at] == number)
+        def _(source=source):
+            copy(source, target, sem).start()
+
+
+def settle(cases, who_ref, target, sem):
+    held = functools.reduce(jnp.logical_or, [who_ref[at] == number for at, number, _ in cases])
+
+    @pl.when(held)
     def _():
-        for i, strip in enumerate(strips):
-            c, upto = i * STRIP, (i + 1) * STRIP
-            high_ref[c:upto, :upto], low_ref[c:upto, :upto] = halves(strip[...])
-
-    for c in range(0, P_SIZE, STRIP):
-        upto = c + STRIP
-        a, b = halves(rows_ref[:, :upto])
-        high, low = high_ref[c:upto, :upto], low_ref[c:upto, :upto]
-        part = mm(a, high, NT) + (mm(a, low, NT) + mm(b, high, NT))
-        out_high_ref[:, c:upto], out_low_ref[:, c:upto] = halves(part)
-
-
-def solve(rows, strips):
-    step = min(512, rows.shape[0])
-    part = pl.BlockSpec((step, P_SIZE), lambda i: (i, 0))
+        copy(target, target, sem).wait()
+
+
+def view(ref, first, shape):
+    return ref.at[pl.ds(first, shape[0]), pl.ds(0, shape[1])]
+
+
+def solve_kernel(count, base, outer, plan, strip_plan, who_ref, token_ref, rows_ref, high_in, low_in, *refs):
+    sources = refs[:count]
+    out_high_ref, out_low_ref, raw_ref, inv_ref, high_ref, low_ref, piece_sem, strip_sem = refs[count:]
+
+    def of(cases, shape):
+        return [(at, n, view(sources[ref], f, shape)) for at, n, ref, f in cases]
+
+    for k, (first, shape, cases) in enumerate(strip_plan):
+        pick(of(cases, shape), who_ref, view(inv_ref, first, shape), strip_sem.at[k])
+    for k, (first, shape, cases) in enumerate(plan):
+        pick(of(cases, shape), who_ref, view(raw_ref, first - base, shape), piece_sem.at[k])
+    for k, (first, shape, cases) in enumerate(strip_plan):
+        target = view(inv_ref, first, shape)
+        copy(target, target, strip_sem.at[k]).wait()
+        part = (slice(first, first + shape[0]), slice(0, shape[1]))
+        high_ref[part], low_ref[part] = halves(inv_ref[part])
+    for k, (first, shape, cases) in enumerate(plan):
+        settle(of(cases, shape), who_ref, view(raw_ref, first - base, shape), piece_sem.at[k])
+
+    def part(i, _):
+        rows = pl.ds(pl.multiple_of(i * STRIP, STRIP), STRIP)
+        place = lax.broadcasted_iota(jnp.int32, (STRIP, rows_ref.shape[1]), 0) + i * STRIP + base
+        onehot = jnp.where(place == rows_ref[...], 1.0, 0.0).astype(BF16)
+        raw = raw_ref[rows, :] + (mm(onehot, high_in[...], NT) + mm(onehot, low_in[...], NT))
+        a, b = halves(raw)
+        for c in range(0, P_SIZE, STRIP):
+            upto = c + STRIP
+            high, low = high_ref[c:upto, :upto], low_ref[c:upto, :upto]
+            total = mm(a[:, :upto], high, NT) + (mm(a[:, :upto], low, NT) + mm(b[:, :upto], high, NT))
+            out_high_ref[rows, c:upto], out_low_ref[rows, c:upto] = halves(total)
+        return 0
+
+    start = jnp.where(who_ref[outer] == 0, max(0, P_SIZE - base) // STRIP, 0)
+    lax.fori_loop(jnp.minimum(start, raw_ref.shape[0] // STRIP), raw_ref.shape[0] // STRIP, part, 0)
+
+
+def solve(who, token, outer, rows, expanded, span, plan, strip_plan, arrays):
+    base, count = span[0], span[1] - span[0]
+    used = sorted({case[2] for _, _, cases in plan + strip_plan for case in cases})
+    place = {ref: at for at, ref in enumerate(used)}
+
+    def renumber(entries):
+        return [
+            (first, shape, [(at, n, place[ref], f) for at, n, ref, f in cases])
+            for first, shape, cases in entries
+        ]
+
+    anywhere = pl.BlockSpec(memory_space=pl.ANY)
+    resident = pl.BlockSpec(memory_space=VMEM)
     return pl.pallas_call(
-        solve_kernel,
-        grid=(rows.shape[0] // step,),
-        out_shape=[jax.ShapeDtypeStruct(rows.shape, BF16)] * 2,
-        in_specs=[part] + [pl.BlockSpec(strip.shape, lambda i: (0, 0)) for strip in strips],
-        out_specs=[part, part],
-        scratch_shapes=[VMEM((P_SIZE, P_SIZE), BF16)] * 2,
-        compiler_params=pltpu.CompilerParams(vmem_limit_bytes=40 * MIB),
+        functools.partial(solve_kernel, len(used), base, outer, renumber(plan), renumber(strip_plan)),
+        out_shape=[jax.ShapeDtypeStruct((count, P_SIZE), BF16)] * 2,
+        in_specs=[pl.BlockSpec(memory_space=pltpu.SMEM), anywhere]
+        + [resident] * 3
+        + [anywhere] * len(used),
+        out_specs=[resident] * 2,
+        scratch_shapes=[
+            VMEM((count, P_SIZE), F32),
+            VMEM((P_SIZE, P_SIZE), F32),
+            VMEM((P_SIZE, P_SIZE), BF16),
+            VMEM((P_SIZE, P_SIZE), BF16),
+            pltpu.SemaphoreType.DMA((len(plan),)),
+            pltpu.SemaphoreType.DMA((len(strip_plan),)),
+        ],
+        compiler_params=pltpu.CompilerParams(vmem_limit_bytes=58 * MIB),
+        cost_estimate=pl.CostEstimate(flops=2 * 10**10, bytes_accessed=2 * 10**7, transcendentals=0),
         name="solve_rows",
-    )(rows, *strips)
-
-
-def update_kernel(step, place_ref, rh_ref, rl_ref, ch_ref, cl_ref, front_ref, factor_ref, out_ref):
-    above = (place_ref[0] == 0) & (pl.program_id(0) * step < P_SIZE)
-    first_col = place_ref[1] == 0
+    )(who, token, rows, *expanded, *[arrays[ref] for ref in used])
+
+
+def update_kernel(step, first_row, first_col, who_ref, rh_ref, rl_ref, ch_ref, cl_ref, front_ref, factor_ref, out_ref):
+    above = (who_ref[0] == 0) & (pl.program_id(0) * step + first_row < P_SIZE)
     width = out_ref.shape[1]
 
     def schur(left):
@@ -328,78 +435,147 @@
             part = mm(a, high, NT) + (mm(a, low, NT) + mm(b, high, NT))
             out_ref[:, c : c + WIDE] = front_ref[:, c : c + WIDE] - part
 
+    panel = (who_ref[1] == 0) if first_col == 0 else False
+
     @pl.when(above)
     def _():
         out_ref[...] = front_ref[...]
 
-        @pl.when(first_col)
+    if first_col == 0:
+
+        @pl.when(above & panel)
         def _():
             out_ref[:, :P_SIZE] = factor_ref[...]
 
-    @pl.when(jnp.logical_not(above) & first_col)
-    def _():
-        out_ref[:, :P_SIZE] = rh_ref[...].astype(F32) + rl_ref[...].astype(F32)
-        schur(P_SIZE)
-
-    @pl.when(jnp.logical_not(above) & jnp.logical_not(first_col))
+        @pl.when(jnp.logical_not(above) & panel)
+        def _():
+            out_ref[:, :P_SIZE] = rh_ref[...].astype(F32) + rl_ref[...].astype(F32)
+            schur(P_SIZE)
+
+    @pl.when(jnp.logical_not(above) & jnp.logical_not(panel))
     def _():
         schur(0)
 
 
-def update(place, row_parts, col_parts, front, factor_rows):
-    step = 256
-    count, width = front.shape
+def update(who, row_parts, col_parts, first_row, first_col, front, factor_rows):
+    step = STRIP
+    tall, wide = row_parts[0].shape[0], col_parts[0].shape[0]
     row = pl.BlockSpec((step, P_SIZE), lambda i: (i, 0))
-    whole = pl.BlockSpec((width, P_SIZE), lambda i: (0, 0))
-    wide = pl.BlockSpec((step, width), lambda i: (i, 0))
+    whole = pl.BlockSpec((wide, P_SIZE), lambda i: (0, 0))
+    block = pl.BlockSpec((step, wide), lambda i: (i + first_row // step, first_col // wide))
     last = P_SIZE // step - 1
     return pl.pallas_call(
-        functools.partial(update_kernel, step),
-        grid=(count // step,),
-        out_shape=jax.ShapeDtypeStruct((count, width), F32),
+        functools.partial(update_kernel, step, first_row, first_col),
+        grid=(tall // step,),
+        out_shape=jax.ShapeDtypeStruct(front.shape, F32),
         in_specs=[
             pl.BlockSpec(memory_space=pltpu.SMEM),
             row,
             row,
             whole,
             whole,
-            wide,
-            pl.BlockSpec((step, P_SIZE), lambda i: (jnp.minimum(i, last), 0)),
+            block,
+            pl.BlockSpec((step, P_SIZE), lambda i: (jnp.minimum(i + first_row // step, last), 0)),
         ],
-        out_specs=wide,
-        compiler_params=pltpu.CompilerParams(vmem_limit_bytes=56 * MIB),
+        out_specs=block,
+        input_output_aliases={5: 0},
+        compiler_params=pltpu.CompilerParams(vmem_limit_bytes=58 * MIB),
         name="schur_update",
-    )(place, *row_parts, *col_parts, front, factor_rows)
-
-
-def pairs_of(route, rows, cols, col_count):
-    return [
-        (r * col_count + c, to[0] * col_count + to[1])
-        for r in rows
-        for c in cols
-        for to in [route(r, c)]
-        if to is not None
-    ]
-
-
-def down_columns(part, col, rows):
-    moves = [[(r * 4 + a, r * 4 + b) for r in rows] for a, b in ((0, 2), (2, 1), (2, 3))]
-    middle = lax.ppermute(part, GRID, moves[0])
-    one = lax.ppermute(middle, GRID, moves[1])
-    three = lax.ppermute(middle, GRID, moves[2])
-    return jnp.where(col == 0, part, jnp.where(col == 2, middle, jnp.where(col == 1, one, three)))
-
-
-def in_plane(part, row, col, cols, source, hops):
-    held = part
-    result = part
-    at = 0
-    for hop in hops:
-        pairs = [((source(c) ^ at) * 4 + c, (source(c) ^ at ^ hop) * 4 + c) for c in cols]
-        held = lax.ppermute(held, GRID, pairs)
-        at ^= hop
-        result = jnp.where(row == (source(col) ^ at), held, result)
-    return result
+    )(who, *row_parts, *col_parts, front, factor_rows)
+
+
+BUFFER = 272
+CARRIER = 2
+FIRST = 1536
+STRIPS = (512, 256, 256)
+TOP_STEP = 1
+TOP_END = 5
+FACTOR_STEP = 2
+INVERSE_ENDS = (5, 6, 7)
+ASSEMBLE_STEP = 3
+EXPAND_STEP = 9
+SOLVE_STEP = 10
+GATE_VMEM = 58
+
+
+def move(part, pairs):
+    return lax.ppermute(part, GRID, [(a * 4 + b, c * 4 + d) for (a, b), (c, d) in pairs])
+
+
+def gate_kernel(fresh, held, who_ref, *refs):
+    outs = refs[held : held + 1 + len(fresh)]
+    stages, sems = refs[held + 1 + len(fresh) : -1], refs[-1]
+    outs[0][...] = jnp.zeros_like(outs[0])
+
+    def each(action):
+        at = 0
+        for k, (_, segments) in enumerate(fresh):
+            for first, shape, cases in segments:
+                action(k, at, first, shape, cases)
+                at += 1
+
+    def load(k, at, first, shape, cases):
+        sources = [(where, n, view(refs[ref], f, shape)) for where, n, ref, f in cases]
+        pick(sources, who_ref, view(stages[k], first, shape), sems.at[at])
+
+    def loaded(k, at, first, shape, cases):
+        settle([case[:3] for case in cases], who_ref, view(stages[k], first, shape), sems.at[at])
+
+    def store(k, at, first, shape, cases):
+        for where, n, _, _ in cases:
+
+            @pl.when(who_ref[where] == n)
+            def _():
+                copy(view(stages[k], first, shape), view(outs[1 + k], first, shape), sems.at[at]).start()
+
+    each(load)
+    each(loaded)
+    each(store)
+    each(loaded)
+
+
+class Line:
+    def __init__(self, who):
+        self.who = who
+        self.token = jnp.zeros((8, 128), F32)
+
+    def gate(self, arrived, fresh=()):
+        arrays = [self.token] + list(arrived)
+
+        def place(array):
+            for k, other in enumerate(arrays):
+                if other is array:
+                    return k
+            arrays.append(array)
+            return len(arrays) - 1
+
+        entries = [
+            (shape, [(f, size, [(at, n, place(a), r) for at, n, a, r in cases]) for f, size, cases in segments])
+            for shape, segments in fresh
+        ]
+        anywhere = pl.BlockSpec(memory_space=pl.ANY)
+        parts = max(1, sum(len(segments) for _, segments in entries))
+        out = pl.pallas_call(
+            functools.partial(gate_kernel, entries, len(arrays)),
+            out_shape=[jax.ShapeDtypeStruct((8, 128), F32)]
+            + [jax.ShapeDtypeStruct(shape, F32) for shape, _ in entries],
+            in_specs=[pl.BlockSpec(memory_space=pltpu.SMEM)] + [anywhere] * len(arrays),
+            out_specs=[pl.BlockSpec(memory_space=VMEM)] + [anywhere] * len(entries),
+            scratch_shapes=[VMEM(shape, F32) for shape, _ in entries] + [pltpu.SemaphoreType.DMA((parts,))],
+            compiler_params=pltpu.CompilerParams(vmem_limit_bytes=GATE_VMEM * MIB),
+            name="gate",
+        )(self.who, *arrays)
+        self.token = out[0]
+        return out[1:]
+
+
+def pieces_of(rows, tile_rows):
+    sizes, left = [], rows
+    while left > 0:
+        room = BUFFER - tile_rows if len(sizes) == CARRIER else BUFFER
+        sizes.append(min(room, left))
+        left -= sizes[-1]
+    return sizes
 
 
 def fast_local(front_block, child_tiles, child_rows, child_cols, child_owner):
@@ -407,40 +583,287 @@
     block_rows, block_cols = front.shape
     row = lax.axis_index("row")
     col = lax.axis_index("col")
+    away = row ^ col
+    low = (1, 2, 3)
+    bottom = block_rows - P_SIZE
+    yes = lambda flag: jnp.where(flag, 1, 0)
+    mine = row * 4 + col
+    along = jnp.where(col == 0, yes(row > 0), jnp.where((row == 0) & (col == 1), 3, jnp.where(col < 3, 2, 0)))
+    round_zero = jnp.where(row == 1, 3, jnp.where(row == 3, 2, 0))
+    round_low = jnp.where(away == 0, 1, jnp.where(away == 1, 2, 0))
+    who = jnp.stack(
+        [
+            row,
+            col,
+            mine,
+            yes(mine == 0),
+            along,
+            jnp.where(col == 0, round_zero, round_low),
+            jnp.where(row == 0, col, 4),
+            jnp.where(col == 0, 0, mine),
+        ]
+    ).astype(jnp.int32)
+    line = Line(who)
+    arrays = [front]
+
+    def use(array):
+        for ref, other in enumerate(arrays):
+            if other is array:
+                return ref
+        arrays.append(array)
+        return len(arrays) - 1
+
+    known = {}
+    ends = {}
+    steps = {}
+
+    def until(step, *moved):
+        ends.setdefault(step, []).extend(moved)
+
+    def do(step, action):
+        steps.setdefault(step, []).append(action)
+
     slots = pack(child_tiles[0], child_rows[0], child_cols[0], child_owner[0], 16)
     slots = lax.all_to_all(slots, GRID, split_axis=0, concat_axis=0, tiled=True)
-    rows = slots[:, CR + 1, :CR].astype(jnp.int32).reshape(1, -1)
-    high, low = expand(slots, block_cols)
-    assembled = assemble(front, rows, high, low)
-    holds = ((row == 0) & (col == 0)).astype(jnp.int32)
-    factor_rows, inverse = factor(assembled[:P_SIZE, :P_SIZE], holds)
-    strips = []
-    for c in range(0, P_SIZE, STRIP):
-        strip = inverse[c : c + STRIP, : c + STRIP]
-        strip = down_columns(strip, col, (0,))
-        one = lax.ppermute(strip, GRID, [(c, 4 + c) for c in range(4)])
-        two = lax.ppermute(strip, GRID, [(c, 8 + c) for c in range(4)])
-        three = lax.ppermute(one, GRID, [(4 + c, 12 + c) for c in range(4)])
-        strip = jnp.where(row == 0, strip, jnp.where(row == 1, one, jnp.where(row == 2, two, three)))
-        strips.append(strip)
-    size = block_rows // CHUNKS
-    row_chunks, col_chunks = [], []
-    for at in range(CHUNKS):
-        top = at * size
-        part = assembled[top : top + size, :P_SIZE]
-        top_rows = top < P_SIZE
-        part = down_columns(part, col, (1, 2, 3) if top_rows else (0, 1, 2, 3))
-        row_chunks.append(part)
-        half = size // 2
-        cols = (1, 2, 3) if top_rows else (0, 1, 2, 3)
-        source = lambda c: c
-        first = in_plane(part[:half], row, col, cols, source, (1, 2, 1))
-        second = in_plane(part[half:], row, col, cols, source, (2, 1, 2))
-        col_chunks += [first, second]
-    row_solved = solve(jnp.concatenate(row_chunks, 0), strips)
-    col_solved = solve(jnp.concatenate(col_chunks, 0), strips)
-    place = jnp.stack([row, col]).astype(jnp.int32)
-    return update(place, row_solved, col_solved, assembled, factor_rows)[None]
+    flat = slots.reshape(-1, P_SIZE)
+    tile_rows = flat.shape[0]
+
+    def rows_of(array):
+        return array[:, CR + 1, :CR].astype(jnp.int32).reshape(1, -1)
+
+    plans = {"row": [], "col": []}
+    tiles = {"row": [(7, 0, flat, 0)], "col": [(2, 0, flat, 0)]}
+
+    def found(name, first, rows, where, number, array, inner):
+        plans[name].append((first, rows, where, number, array, inner))
+
+    sizes = pieces_of(block_rows, tile_rows)
+    count = len(sizes)
+    tops = [sum(sizes[:k]) for k in range(count)]
+    found("row", 0, block_rows, 7, 0, front, 0)
+    found("col", bottom, P_SIZE, 2, 0, front, bottom)
+    zero_rows = P_SIZE + tile_rows
+    zero_count = -(-zero_rows // BUFFER)
+    hops = {"z": {}, "xd": {}, "y": {}}
+
+    def arrived_low(k):
+        def hold(name, number, array):
+            found(name, tops[k], sizes[k], 2, number, array, 0)
+            if k == CARRIER:
+                tiles[name].append((2, number, array, sizes[k]))
+
+        for r in low:
+            for c in low:
+                hold("row", r * 4 + c, hops["z"][k + c - 1])
+        for c in low:
+            hold("col", c * 4 + c, hops["z"][k + c - 1])
+            hold("col", (c ^ 1) * 4 + c, hops["xd"][k + c])
+            hold("col", (c ^ 2) * 4 + c, hops["y"][k + c])
+            hold("col", (c ^ 3) * 4 + c, hops["xd"][k + c + 1])
+
+    zero_hops = {"row": (1, ((2, "z", 0), (3, "z", 1))), "col": (4, ((12, "xd", 0), (8, "xd", 1)))}
+
+    def arrived_zero_tiles():
+        for name, (near, others) in zero_hops.items():
+            tiles[name].append((2, near, known["zero", name], 0))
+            for number, kind, late in others:
+                tiles[name].append((2, number, hops[kind][TOP_END + late], 0))
+
+    def arrived_zero(j):
+        for name, (near, others) in zero_hops.items():
+            first, last = max(0, j * BUFFER - tile_rows), min((j + 1) * BUFFER, zero_rows) - tile_rows
+            inner = first + tile_rows - j * BUFFER
+            found(name, bottom + first, last - first, 2, near, known["zero", name], first + tile_rows)
+            for number, kind, late in others:
+                found(name, bottom + first, last - first, 2, number, hops[kind][TOP_END + j + late], inner)
+
+    def z_fresh(step):
+        segments = []
+        whole = (BUFFER, P_SIZE)
+        if step > 0:
+            segments.append((0, whole, [(4, 2, hops["z"][step - 1], 0)]))
+        if step < count:
+            segments.append((0, (sizes[step], P_SIZE), [(4, 1, front, tops[step])]))
+            if step == CARRIER:
+                segments.append((sizes[step], (tile_rows, P_SIZE), [(4, 1, flat, 0)]))
+        segments += zero_segments(step, "row", 4)
+        return (whole, segments)
+
+    def zero_segments(step, name, place):
+        j = step - TOP_END
+        if 0 <= j < zero_count:
+            tall = min(BUFFER, zero_rows - j * BUFFER)
+            return [(0, (tall, P_SIZE), [(place, 3, known["zero", name], j * BUFFER)])]
+        return []
+
+    def xd_fresh(step):
+        whole = (BUFFER, P_SIZE)
+        segments = [(0, whole, [(5, 1, hops["z"][step - 1], 0)])]
+        if step - 1 in hops["xd"]:
+            segments.append((0, whole, [(5, 2, hops["xd"][step - 1], 0)]))
+        return (whole, segments + zero_segments(step, "col", 5))
+
+    def z_move(step, part):
+        pairs = []
+        for c in range(3):
+            if 0 <= step - c < count:
+                pairs += [((r, c), (r, c + 1)) for r in low]
+            if c > 0 and 0 <= step - (c - 1) - TOP_END < zero_count:
+                pairs.append(((0, c), (0, c + 1)))
+        hops["z"][step] = move(part, pairs)
+        until(step + 1, hops["z"][step])
+
+    def xd_move(step, part):
+        pairs = []
+        for c in low:
+            if 0 <= step - c < count:
+                pairs.append(((c, c), (c ^ 1, c)))
+            if 0 <= step - c - 1 < count:
+                pairs.append(((c ^ 1, c), (c ^ 3, c)))
+        if 0 <= step - TOP_END < zero_count:
+            pairs.append(((1, 0), (3, 0)))
+        if 0 <= step - 1 - TOP_END < zero_count:
+            pairs.append(((3, 0), (2, 0)))
+        hops["xd"][step] = move(part, pairs)
+        until(step + 1, hops["xd"][step])
+
+    def y_move(step):
+        pairs = [((c, c), (c ^ 2, c)) for c in low if 0 <= step - c < count]
+        if pairs:
+            hops["y"][step] = move(hops["z"][step - 1], pairs)
+            until(step + 1, hops["y"][step])
+
+    def top(part):
+        known["zero", "row"] = move(part, [((0, 0), (0, 1))])
+        known["zero", "col"] = move(part, [((0, 0), (1, 0))])
+        until(TOP_END, known["zero", "row"], known["zero", "col"])
+
+    holds = yes(mine == 0).reshape(1)
+    strip_plan = []
+    wanted = {}
+
+    def factoring():
+        known["rows"] = rows_of(slots)
+        panel = expand(slots, P_SIZE, line.token)
+        state = [front, known["rows"], *panel]
+        for at, tall in enumerate(STRIPS):
+            first = sum(STRIPS[:at])
+            z_state, known["factor"], strip = factor(first, tall, holds, line.token, state, P_SIZE)
+            state = [z_state, known["factor"]]
+            two = move(strip, [((0, 0), (0, 2))])
+            step = INVERSE_ENDS[at]
+            until(step, two)
+            want(step, strip.shape, [(2, 0, strip, 0), (2, 2, two, 0)], functools.partial(inverse_across, step, first))
+
+    def want(step, shape, cases, action):
+        wanted.setdefault(step, []).append(((shape, [(0, shape, cases)]), action))
+
+    def inverse_across(step, first, part):
+        other = move(part, [((0, 0), (0, 1)), ((0, 2), (0, 3))])
+        until(step + 1, other)
+        cases = [(6, c, (part, other)[c % 2], 0) for c in range(4)]
+        want(step + 1, part.shape, cases, functools.partial(inverse_plane, step + 1, first))
+
+    def inverse_plane(step, first, part):
+        near = move(part, [((0, c), (1, c)) for c in range(4)])
+        until(step + 1, near)
+        cases = [(0, 0, part, 0), (0, 1, near, 0)]
+        want(step + 1, part.shape, cases, functools.partial(inverse_far, step + 1, first))
+
+    def inverse_far(step, first, part):
+        far = move(part, [((r, c), (r + 2, c)) for r in (0, 1) for c in range(4)])
+        until(step + 1, far)
+        strip_plan.append((first, part.shape, [(0, r, use((part, far)[r // 2]), 0) for r in range(4)]))
+
+    def assembling():
+        parts = expand(slots, block_cols, line.token)
+        known["assembled"] = assemble(front, known["rows"], *parts, line.token)
+
+    def expanding(row_part, col_part):
+        for name, part in (("row", row_part), ("col", col_part)):
+            own = part.reshape(slots.shape)
+            known[name] = (rows_of(own), expand(own, P_SIZE, line.token))
+
+    groups = (0, FIRST, block_rows)
+    solved = {}
+
+    def solving(group, name):
+        low_end, high_end = groups[group], groups[group + 1]
+        plan = {}
+        for first, rows, where, number, array, inner in plans[name]:
+            a, b = max(first, low_end), min(first + rows, high_end)
+            if a < b:
+                plan.setdefault((a, b), []).append((where, number, use(array), inner + a - first))
+        entries = [(a, (b - a, P_SIZE), cases) for (a, b), cases in plan.items()]
+        outer = 0 if name == "row" else 1
+        solved[name, group] = solve(
+            who, line.token, outer, *known[name], (low_end, high_end), entries, strip_plan, arrays
+        )
+
+    def updating(a, b):
+        known["assembled"] = update(
+            who, solved["row", a], solved["col", b], groups[a], groups[b], known["assembled"], known["factor"]
+        )
+
+    last = max(count + 4, TOP_END + zero_count + 1)
+    for step in range(last + 1):
+        fresh, uses = [], []
+
+        def wants(entry, action):
+            fresh.append(entry)
+            uses.append(action)
+
+        if step < max(count + 2, TOP_END + zero_count + 1):
+            wants(z_fresh(step), functools.partial(z_move, step))
+        if 0 < step < last:
+            wants(xd_fresh(step), functools.partial(xd_move, step))
+        if step == TOP_STEP:
+            segments = [(0, (tile_rows, P_SIZE), [(3, 1, flat, 0)])]
+            segments.append((tile_rows, (P_SIZE, P_SIZE), [(3, 1, front, bottom)]))
+            wants(((zero_rows, P_SIZE), segments), top)
+        for entry, action in wanted.get(step, []):
+            wants(entry, action)
+        if step == EXPAND_STEP:
+            arrived_low(CARRIER)
+            arrived_zero_tiles()
+            for name in ("row", "col"):
+                shape = (tile_rows, P_SIZE)
+                wants((shape, [(0, shape, tiles[name])]), lambda part, name=name: known.__setitem__(("tiles", name), part))
+        out = line.gate(ends.get(step, []), fresh)
+        for part, action in zip(out, uses):
+            action(part)
+        if 0 < step < last:
+            y_move(step)
+        for action in steps.get(step, []):
+            action()
+        if step == FACTOR_STEP:
+            factoring()
+        if step == ASSEMBLE_STEP:
+            assembling()
+            until(step + 1, known["assembled"])
+        if step == EXPAND_STEP:
+            expanding(known["tiles", "row"], known["tiles", "col"])
+        if step == SOLVE_STEP:
+            for k in range(count):
+                if k != CARRIER and tops[k] < FIRST:
+                    arrived_low(k)
+            early = [j for j in range(zero_count) if bottom + j * BUFFER - tile_rows < FIRST]
+            for j in early:
+                arrived_zero(j)
+            solving(0, "row")
+            solving(0, "col")
+    for k in range(count):
+        if tops[k] >= FIRST:
+            arrived_low(k)
+    for j in range(len(early), zero_count):
+        arrived_zero(j)
+    updating(0, 0)
+    solving(1, "row")
+    solving(1, "col")
+    updating(0, 1)
+    updating(1, 0)
+    updating(1, 1)
+    return known["assembled"][None]
 
 
 def blocked_factor(symmetric):

time: 765 us -> 578 us (0.76)
  starting transfers between devices: 321 us -> 67.9 us
  Pallas kernels: 81.7 us -> 198 us
  other arithmetic: 42.6 us -> 1.15 us
  waiting for transfers between devices: 282 us -> 245 us
  blocking collectives: 0 us -> 31.7 us
    ppermute x96 -> x46, starting transfers between devices: 314 us -> 67.9 us  [move(): lax.ppermute(part, GRID, [(a * 4 + b, c * 4 + d) for (a, b), (c, d) in pa...]
    pallas_call x4 -> x24, Pallas kernels: 56.8 us -> 155 us  [the longest x4 61 us: solve(): pl.pallas_call(functools.partial(solve_kernel, len(used), base, outer, re...]
    all_to_all x0 -> x1, blocking collectives: none -> 31.7 us  [fast_local(): slots = lax.all_to_all(slots, GRID, split_axis=0, concat_axis=0, tiled=True)]
    unnamed x22 -> x0, other arithmetic: 30 us -> none
    ppermute x96 -> x46, waiting for transfers between devices: 271 us -> 245 us  [move(): lax.ppermute(part, GRID, [(a * 4 + b, c * 4 + d) for (a, b), (c, d) in pa...]
    pallas_call x1 -> x4, Pallas kernels: 6.01 us -> 22.6 us  [expand(): pl.pallas_call(expand_kernel, grid=(count // 8,), out_shape=[jax.ShapeDty...]
    all_to_all x1 -> x0, waiting for transfers between devices: 10.6 us -> none  [fast_local(): slots = lax.all_to_all(slots, GRID, split_axis=0, concat_axis=0, tiled=True)]
    slice x14 -> x0, local copies, waits for them, and re-layouts: 9.96 us -> none  [the longest x8 4.5 us: fast_local(): second = in_plane(part[half:], row, col, cols, source, (2, 1, 2))]
  transfers between devices with their start and end apart: 97 -> 46, of which waited for: 19 -> 13; matrix products, arithmetic and copies ran while one was open for 7% -> 1% of each run, Pallas kernels for 2% -> 22%
where the time goes in v2:
time: 578 us; the launch traced here: 573 us
  waiting for transfers between devices  245 us (42%)
  Pallas kernels  198 us (34%)
  starting transfers between devices  67.9 us (12%)
  blocking collectives  31.7 us (5%)
  local copies, waits for them, and re-layouts  27.8 us (5%)
    ppermute x46, waiting for transfers between devices, move(): lax.ppermute(part, GRID, [(a * 4 + b, c * 4 + d) for (a, b), (c, d) in pa...  245 us
    ppermute x46, starting transfers between devices, move(): lax.ppermute(part, GRID, [(a * 4 + b, c * 4 + d) for (a, b), (c, d) in pa...  67.9 us
    pallas_call x4, Pallas kernels, solve(): pl.pallas_call(functools.partial(solve_kernel, len(used), base, outer, re...  61 us
    pallas_call x4, Pallas kernels, update(): pl.pallas_call(functools.partial(update_kernel, step, first_row, first_co...  49 us
    pallas_call x13, Pallas kernels, gate(): pl.pallas_call(functools.partial(gate_kernel, entries, len(arrays)), out_...  40.1 us
    all_to_all x1, blocking collectives, fast_local(): slots = lax.all_to_all(slots, GRID, split_axis=0, concat_axis=0, tiled=True)  31.7 us
    pallas_call x4, Pallas kernels, expand(): pl.pallas_call(expand_kernel, grid=(count // 8,), out_shape=[jax.ShapeDty...  22.6 us
    unnamed x87, local copies, waits for them, and re-layouts  19.4 us
  transfers between devices with their start and end apart: 46, of which 13 were waited for; matrix products, arithmetic and copies ran while one was open for 1% of the time, Pallas kernels for 22%

profile of v2, /device:TPU:12, one launch (start us, length us, event | category | flops | bytes accessed | tf_op | source)
XLA Modules:
  0.0 573.3 jit_solution(1337861490614008096)
XLA Ops:
  4.6 1.8 pack_tiles.1
  6.5 31.7 %all_to_all.5.slots_ref = f32[32,24,128]{2,1,0:T(8,128)S(1)} all-to-all(f32[32,24,128]{2,1,0:T(8,128)} %pack_tiles.1), channel_id=1, replica_groups=mesh['front'=2,'row'=4,'col'=4] {'row','col'}, dimensions={0} | all-to-all | bytes 786432 | tf_op jit(solution)/shard_map/all_to_all | solution.py:627
  40.0 3.5 gate.14
  43.6 3.8 collective-permute-start.1
  48.9 2.8 collective-permute-start.10
  51.7 2.9 collective-permute-start.11
  54.6 16.1 %collective-permute-done.1.refs_1_.refs_11_ = f32[272,1024]{1,0:T(8,128)S(1)} collective-permute-done((f32[272,1024]{1,0:T(8,128)}, f32[272,1024]{1,0:T(8,128)S(1)}, u32[]{:S(2)}, u32[]{:S(2)}) %collective-permute-start.1) | collective-permute-done | bytes 1114144 | tf_op jit(solution)/shard_map/ppermute | solution.py:502
  72.4 3.5 gate.15
  75.9 5.0 collective-permute-start.4
  83.0 20.3 %collective-permute-done.4.refs_1_.refs_10_.refs_7_ = f32[272,1024]{1,0:T(8,128)S(1)} collective-permute-done((f32[272,1024]{1,0:T(8,128)}, f32[272,1024]{1,0:T(8,128)S(1)}, u32[]{:S(2)}, u32[]{:S(2)}) %collective-permute-start.4) | collective-permute-done | bytes 1114144 | tf_op jit(solution)/shard_map/ppermute | solution.py:502
  103.3 4.0 collective-permute-done.5.refs_2_.refs_24_
  108.7 3.5 gate.16
  112.2 2.3 collective-permute-start.7
  115.2 5.1 expand_columns.5
  122.4 4.6 panel_factor.3
  127.0 10.6 %collective-permute-done.7.refs_1_.refs_11_.refs_8_ = f32[272,1024]{1,0:T(8,128)S(1)} collective-permute-done((f32[272,1024]{1,0:T(8,128)}, f32[272,1024]{1,0:T(8,128)S(1)}, u32[]{:S(2)}, u32[]{:S(2)}) %collective-permute-start.7) | collective-permute-done | bytes 1114144 | tf_op jit(solution)/shard_map/ppermute | solution.py:502
  139.3 7.3 %expand_columns.4 = (bf16[2048,512]{1,0:T(8,128)(2,1)}, bf16[2048,512]{1,0:T(8,128)(2,1)}) custom-call(f32[8,128]{1,0:T(8,128)} %get-tuple-element.83.token_ref.refs_0_, f32[32,24,128]{2,1,0:T(8,128)} %copy-done), custom_call_target="tpu_custom_call" | custom-call | tf_op jit(solution)/shard_map/expand_columns/pallas_call | solution.py:290
  146.6 18.3 %assemble.1.refs_4_.front_ref = f32[2048,2048]{1,0:T(8,128)} custom-call(f32[8,128]{1,0:T(8,128)} %get-tuple-element.83.token_ref.refs_0_, s32[1,512]{1,0:T(1,128)} %convert_element_type.40.rows_ref.refs_1_, bf16[2048,512]{1,0:T(8,128)(2,1)} %get-tuple-element.86.high_ref, bf16[2048,512]{1,0:T(8,128)(2,1)} %get-tuple-element.87.low_ref, f32[2048,2048]{1,0:T(8,128)} %bitcast.21), custom_call_target="tpu_custom_call" | custom-call | tf_op jit(solution)/shard_map/assemble/pallas_call | solution.py:312
  167.1 3.6 gate.17
  170.7 3.3 collective-permute-start.13
  176.3 18.9 %collective-permute-done.13.refs_4_.refs_12_.refs_9_ = f32[272,1024]{1,0:T(8,128)S(1)} collective-permute-done((f32[272,1024]{1,0:T(8,128)}, f32[272,1024]{1,0:T(8,128)S(1)}, u32[]{:S(2)}, u32[]{:S(2)}) %collective-permute-start.13) | collective-permute-done | bytes 1114144 | tf_op jit(solution)/shard_map/ppermute | solution.py:502
  200.3 3.6 gate.18
  203.9 6.0 %collective-permute-start.17 = (f32[272,1024]{1,0:T(8,128)}, f32[272,1024]{1,0:T(8,128)S(1)}, u32[]{:S(2)}, u32[]{:S(2)}) collective-permute-start(f32[272,1024]{1,0:T(8,128)} %get-tuple-element.99), channel_id=1, source_target_pairs={{4,5},{8,9},{12,13},{5,6},{9,10},{13,14},{1,2},{6,7},{10,11},{14,1... | collective-permute-start | bytes 3342344 | tf_op jit(solution)/shard_map/ppermute | solution.py:502
  214.1 13.3 %collective-permute-done.17.refs_2_.refs_13_.refs_12_ = f32[272,1024]{1,0:T(8,128)S(1)} collective-permute-done((f32[272,1024]{1,0:T(8,128)}, f32[272,1024]{1,0:T(8,128)S(1)}, u32[]{:S(2)}, u32[]{:S(2)}) %collective-permute-start.17) | collective-permute-done | bytes 1114144 | tf_op jit(solution)/shard_map/ppermute | solution.py:502
  227.5 3.2 collective-permute-done.18.refs_3_.refs_19_
  231.7 3.6 gate.19
  235.4 1.9 collective-permute-start.22
  240.9 14.4 %collective-permute-done.22.refs_2_.refs_14_.refs_7_.refs_13_ = f32[272,1024]{1,0:T(8,128)S(1)} collective-permute-done((f32[272,1024]{1,0:T(8,128)}, f32[272,1024]{1,0:T(8,128)S(1)}, u32[]{:S(2)}, u32[]{:S(2)}) %collective-permute-start.22) | collective-permute-done | bytes 1114144 | tf_op jit(solution)/shard_map/ppermute | solution.py:502
  255.2 7.4 %collective-permute-done.23.refs_3_.refs_21_ = f32[272,1024]{1,0:T(8,128)S(1)} collective-permute-done((f32[272,1024]{1,0:T(8,128)}, f32[272,1024]{1,0:T(8,128)S(1)}, u32[]{:S(2)}, u32[]{:S(2)}) %collective-permute-start.23) | collective-permute-done | bytes 1114144 | tf_op jit(solution)/shard_map/ppermute | solution.py:502
  264.0 3.6 gate.20
  268.3 2.6 collective-permute-start.27
  275.1 65.2 %collective-permute-done.31.refs_5_.refs_2_ = f32[512,512]{1,0:T(8,128)S(1)} collective-permute-done((f32[512,512]{1,0:T(8,128)}, f32[512,512]{1,0:T(8,128)S(1)}, u32[]{:S(2)}, u32[]{:S(2)}) %collective-permute-start.31) | collective-permute-done | bytes 1048608 | tf_op jit(solution)/shard_map/ppermute | solution.py:502
  342.3 3.6 gate.21
  351.5 40.3 %collective-permute-done.36.refs_4_ = f32[256,768]{1,0:T(8,128)S(1)} collective-permute-done((f32[256,768]{1,0:T(8,128)}, f32[256,768]{1,0:T(8,128)S(1)}, u32[]{:S(2)}, u32[]{:S(2)}) %collective-permute-start.36) | collective-permute-done | bytes 786464 | tf_op jit(solution)/shard_map/ppermute | solution.py:502
  394.1 4.0 gate.22
  402.2 1.8 reshape.52.slots_ref
  405.9 5.1 expand_columns.6
  410.9 5.1 expand_columns.7
  418.4 29.8 %collective-permute-done.40.refs_3_.refs_6_ = f32[256,1024]{1,0:T(8,128)} collective-permute-done((f32[256,1024]{1,0:T(8,128)}, f32[256,1024]{1,0:T(8,128)}, u32[]{:S(2)}, u32[]{:S(2)}) %collective-permute-start.40) | collective-permute-done | bytes 1048608 | tf_op jit(solution)/shard_map/ppermute | solution.py:502
  450.6 3.5 gate.23
  456.4 20.7 %solve_rows.6 = (bf16[1536,1024]{1,0:T(8,128)(2,1)}, bf16[1536,1024]{1,0:T(8,128)(2,1)}) custom-call(s32[8]{0:T(128)} %stack.35.who_ref, f32[8,128]{1,0:T(8,128)} %get-tuple-element.125.refs_0_.token_ref, s32[1,512]{1,0:T(1,128)} %convert_element_type.44.rows_ref, bf16[1024,512]{1,0:T(8,128)(2,1)} %get-tuple-element.136.high_in, ...), custom_call_target="tpu_custom_call" | custom-call | flops 20000000000 | bytes 20000000 | tf_op jit(solution)/shard_map/solve_rows/pallas_call | solution.py:406
  481.5 20.7 %solve_rows.7 = (bf16[1536,1024]{1,0:T(8,128)(2,1)}, bf16[1536,1024]{1,0:T(8,128)(2,1)}) custom-call(s32[8]{0:T(128)} %stack.35.who_ref, f32[8,128]{1,0:T(8,128)} %get-tuple-element.125.refs_0_.token_ref, s32[1,512]{1,0:T(1,128)} %convert_element_type.42.rows_ref, bf16[1024,512]{1,0:T(8,128)(2,1)} %get-tuple-element.131.high_in, ...), custom_call_target="tpu_custom_call" | custom-call | flops 20000000000 | bytes 20000000 | tf_op jit(solution)/shard_map/solve_rows/pallas_call | solution.py:406
  502.2 21.5 %schur_update.4.front_ref = f32[2048,2048]{1,0:T(8,128)} custom-call(s32[8]{0:T(128)} %stack.35.who_ref, bf16[1536,1024]{1,0:T(8,128)(2,1)} %get-tuple-element.142.rh_ref, bf16[1536,1024]{1,0:T(8,128)(2,1)} %get-tuple-element.143.rl_ref, bf16[1536,1024]{1,0:T(8,128)(2,1)} %get-tuple-element.140.ch_ref, ...), custom_call_target="tpu_custom_call", output_to_operand_aliasing={{}: (5, {})} | custom-call | tf_op jit(solution)/shard_map/schur_update/pallas_call | solution.py:467
  526.0 9.8 %solve_rows.5 = (bf16[512,1024]{1,0:T(8,128)(2,1)}, bf16[512,1024]{1,0:T(8,128)(2,1)}) custom-call(s32[8]{0:T(128)} %stack.35.who_ref, f32[8,128]{1,0:T(8,128)} %gate.25.token_ref, s32[1,512]{1,0:T(1,128)} %convert_element_type.44.rows_ref, bf16[1024,512]{1,0:T(8,128)(2,1)} %get-tuple-element.136.high_in, bf16[1024,512]{1,0:T(8,128)(2,1)} %get-tuple-element.137.low_in, ...), custom_call_target="tpu_custom_call" | custom-call | flops 20000000000 | bytes 20000000 | tf_op jit(solution)/shard_map/solve_rows/pallas_call | solution.py:406
  535.8 11.2 %schur_update.5.front_ref = f32[2048,2048]{1,0:T(8,128)} custom-call(s32[8]{0:T(128)} %stack.35.who_ref, bf16[1536,1024]{1,0:T(8,128)(2,1)} %get-tuple-element.142.rh_ref, bf16[1536,1024]{1,0:T(8,128)(2,1)} %get-tuple-element.143.rl_ref, bf16[512,1024]{1,0:T(8,128)(2,1)} %get-tuple-element.138.ch_ref, ...), custom_call_target="tpu_custom_call", output_to_operand_aliasing={{}: (5, {})} | custom-call | tf_op jit(solution)/shard_map/schur_update/pallas_call | solution.py:467
  547.0 9.8 %solve_rows.4 = (bf16[512,1024]{1,0:T(8,128)(2,1)}, bf16[512,1024]{1,0:T(8,128)(2,1)}) custom-call(s32[8]{0:T(128)} %stack.35.who_ref, f32[8,128]{1,0:T(8,128)} %gate.25.token_ref, s32[1,512]{1,0:T(1,128)} %convert_element_type.42.rows_ref, bf16[1024,512]{1,0:T(8,128)(2,1)} %get-tuple-element.131.high_in, bf16[1024,512]{1,0:T(8,128)(2,1)} %get-tuple-element.132.low_in, ...), custom_call_target="tpu_custom_call" | custom-call | flops 20000000000 | bytes 20000000 | tf_op jit(solution)/shard_map/solve_rows/pallas_call | solution.py:406
  556.8 10.9 %schur_update.6.front_ref = f32[2048,2048]{1,0:T(8,128)} custom-call(s32[8]{0:T(128)} %stack.35.who_ref, bf16[512,1024]{1,0:T(8,128)(2,1)} %get-tuple-element.133.rh_ref, bf16[512,1024]{1,0:T(8,128)(2,1)} %get-tuple-element.134.rl_ref, bf16[1536,1024]{1,0:T(8,128)(2,1)} %get-tuple-element.140.ch_ref, ...), custom_call_target="tpu_custom_call", output_to_operand_aliasing={{}: (5, {})} | custom-call | tf_op jit(solution)/shard_map/schur_update/pallas_call | solution.py:467
  567.6 5.4 schur_update.7
  (174 shorter events, 70.9 us)
Async XLA Ops:
  2.7 36.3 %collective-permute-start = (f32[272,1024]{1,0:T(8,128)}, f32[272,1024]{1,0:T(8,128)S(1)}, u32[]{:S(2)}, u32[]{:S(2)}) collective-permute-start(f32[272,1024]{1,0:T(8,128)} %get-tuple-element.76), channel_id=1, source_target_pairs={{4,5},{8,9},{12,13},{20,21},{24,25},{28,29}} | collective-permute-start | bytes 3342344 | tf_op jit(solution)/shard_map/ppermute | solution.py:502
  38.1 76.4 %copy-start = (f32[32,24,128]{2,1,0:T(8,128)}, f32[32,24,128]{2,1,0:T(8,128)S(1)}, u32[]{:S(2)}) copy-start(f32[32,24,128]{2,1,0:T(8,128)S(1)} %all_to_all.5.slots_ref) | copy-start | bytes 1179652
  43.6 27.1 %collective-permute-start.1 = (f32[272,1024]{1,0:T(8,128)}, f32[272,1024]{1,0:T(8,128)S(1)}, u32[]{:S(2)}, u32[]{:S(2)}) collective-permute-start(f32[272,1024]{1,0:T(8,128)} %get-tuple-element.78), channel_id=1, source_target_pairs={{4,5},{8,9},{12,13},{5,6},{9,10},{13,14},{20,21},{24,25},{28,29},{... | collective-permute-start | bytes 3342344 | tf_op jit(solution)/shard_map/ppermute | solution.py:502
  47.4 23.3 %collective-permute-start.2 = (f32[272,1024]{1,0:T(8,128)}, f32[272,1024]{1,0:T(8,128)S(1)}, u32[]{:S(2)}, u32[]{:S(2)}) collective-permute-start(f32[272,1024]{1,0:T(8,128)} %get-tuple-element.79), channel_id=1, source_target_pairs={{5,1},{21,17}} | collective-permute-start | bytes 3342344 | tf_op jit(solution)/shard_map/ppermute | solution.py:502
  48.2 22.5 %collective-permute-start.3 = (f32[272,1024]{1,0:T(8,128)}, f32[272,1024]{1,0:T(8,128)S(1)}, u32[]{:S(2)}, u32[]{:S(2)}) collective-permute-start(f32[272,1024]{1,0:T(8,128)} %copy-done.14), channel_id=1, source_target_pairs={{5,13},{21,29}} | collective-permute-start | bytes 3342344 | tf_op jit(solution)/shard_map/ppermute | solution.py:502
  48.9 150.4 %collective-permute-start.10 = (f32[1120,1024]{1,0:T(8,128)}, f32[1120,1024]{1,0:T(8,128)}, u32[]{:S(2)}, u32[]{:S(2)}) collective-permute-start(f32[1120,1024]{1,0:T(8,128)} %get-tuple-element.89), channel_id=1, source_target_pairs={{0,1},{16,17}} | collective-permute-start | bytes 13762568 | tf_op jit(solution)/shard_map/ppermute | solution.py:502
  51.7 147.6 %collective-permute-start.11 = (f32[1120,1024]{1,0:T(8,128)}, f32[1120,1024]{1,0:T(8,128)}, u32[]{:S(2)}, u32[]{:S(2)}) collective-permute-start(f32[1120,1024]{1,0:T(8,128)} %get-tuple-element.89), channel_id=1, source_target_pairs={{0,4},{16,20}} | collective-permute-start | bytes 13762568 | tf_op jit(solution)/shard_map/ppermute | solution.py:502
  75.9 27.3 %collective-permute-start.4 = (f32[272,1024]{1,0:T(8,128)}, f32[272,1024]{1,0:T(8,128)S(1)}, u32[]{:S(2)}, u32[]{:S(2)}) collective-permute-start(f32[272,1024]{1,0:T(8,128)} %get-tuple-element.81), channel_id=1, source_target_pairs={{4,5},{8,9},{12,13},{5,6},{9,10},{13,14},{6,7},{10,11},{14,15},{20... | collective-permute-start | bytes 3342344 | tf_op jit(solution)/shard_map/ppermute | solution.py:502
  80.9 26.4 %collective-permute-start.5 = (f32[272,1024]{1,0:T(8,128)}, f32[272,1024]{1,0:T(8,128)S(1)}, u32[]{:S(2)}, u32[]{:S(2)}) collective-permute-start(f32[272,1024]{1,0:T(8,128)} %get-tuple-element.82), channel_id=1, source_target_pairs={{5,1},{1,9},{10,14},{21,17},{17,25},{26,30}} | collective-permute-start | bytes 3342344 | tf_op jit(solution)/shard_map/ppermute | solution.py:502
  82.2 25.1 %collective-permute-start.6 = (f32[272,1024]{1,0:T(8,128)}, f32[272,1024]{1,0:T(8,128)S(1)}, u32[]{:S(2)}, u32[]{:S(2)}) collective-permute-start(f32[272,1024]{1,0:T(8,128)} %copy-done.15), channel_id=1, source_target_pairs={{5,13},{10,2},{21,29},{26,18}} | collective-permute-start | bytes 3342344 | tf_op jit(solution)/shard_map/ppermute | solution.py:502
  112.2 25.4 %collective-permute-start.7 = (f32[272,1024]{1,0:T(8,128)}, f32[272,1024]{1,0:T(8,128)S(1)}, u32[]{:S(2)}, u32[]{:S(2)}) collective-permute-start(f32[272,1024]{1,0:T(8,128)} %get-tuple-element.84), channel_id=1, source_target_pairs={{4,5},{8,9},{12,13},{5,6},{9,10},{13,14},{6,7},{10,11},{14,15},{20... | collective-permute-start | bytes 3342344 | tf_op jit(solution)/shard_map/ppermute | solution.py:502
  120.4 44.6 %collective-permute-start.8 = (f32[272,1024]{1,0:T(8,128)}, f32[272,1024]{1,0:T(8,128)S(1)}, u32[]{:S(2)}, u32[]{:S(2)}) collective-permute-start(f32[272,1024]{1,0:T(8,128)} %get-tuple-element.85), channel_id=1, source_target_pairs={{5,1},{1,9},{10,14},{14,6},{15,11},{21,17},{17,25},{26,30},{30,22}... | collective-permute-start | bytes 3342344 | tf_op jit(solution)/shard_map/ppermute | solution.py:502
  121.7 43.3 %collective-permute-start.9 = (f32[272,1024]{1,0:T(8,128)}, f32[272,1024]{1,0:T(8,128)S(1)}, u32[]{:S(2)}, u32[]{:S(2)}) collective-permute-start(f32[272,1024]{1,0:T(8,128)} %copy-done.1), channel_id=1, source_target_pairs={{5,13},{10,2},{15,7},{21,29},{26,18},{31,23}} | collective-permute-start | bytes 3342344 | tf_op jit(solution)/shard_map/ppermute | solution.py:502
  137.6 37.7 %collective-permute-start.12 = (f32[512,512]{1,0:T(8,128)}, f32[512,512]{1,0:T(8,128)}, u32[]{:S(2)}, u32[]{:S(2)}) collective-permute-start(f32[512,512]{1,0:T(8,128)} %get-tuple-element.92.refs_8_), channel_id=1, source_target_pairs={{0,2},{16,18}} | collective-permute-start | bytes 3145736 | tf_op jit(solution)/shard_map/ppermute | solution.py:502
  170.7 24.5 %collective-permute-start.13 = (f32[272,1024]{1,0:T(8,128)}, f32[272,1024]{1,0:T(8,128)S(1)}, u32[]{:S(2)}, u32[]{:S(2)}) collective-permute-start(f32[272,1024]{1,0:T(8,128)} %get-tuple-element.93), channel_id=1, source_target_pairs={{4,5},{8,9},{12,13},{5,6},{9,10},{13,14},{6,7},{10,11},{14,15},{20... | collective-permute-start | bytes 3342344 | tf_op jit(solution)/shard_map/ppermute | solution.py:502
  174.0 24.5 %collective-permute-start.14 = (f32[272,1024]{1,0:T(8,128)}, f32[272,1024]{1,0:T(8,128)S(1)}, u32[]{:S(2)}, u32[]{:S(2)}) collective-permute-start(f32[272,1024]{1,0:T(8,128)} %get-tuple-element.94), channel_id=1, source_target_pairs={{5,1},{1,9},{10,14},{14,6},{15,11},{11,3},{21,17},{17,25},{26,30},... | collective-permute-start | bytes 3342344 | tf_op jit(solution)/shard_map/ppermute | solution.py:502
  175.3 23.9 %collective-permute-start.15 = (f32[272,1024]{1,0:T(8,128)S(1)}, f32[272,1024]{1,0:T(8,128)S(1)}, u32[]{:S(2)}, u32[]{:S(2)}) collective-permute-start(f32[272,1024]{1,0:T(8,128)S(1)} %copy-done.11), channel_id=1, source_target_pairs={{5,13},{10,2},{15,7},{21,29},{26,18},{31,23}} | collective-permute-start | bytes 3342344 | tf_op jit(solution)/shard_map/ppermute | solution.py:502
  195.2 18.2 %collective-permute-start.16 = (f32[256,768]{1,0:T(8,128)}, f32[256,768]{1,0:T(8,128)}, u32[]{:S(2)}, u32[]{:S(2)}) collective-permute-start(f32[256,768]{1,0:T(8,128)} %get-tuple-element.98.refs_9_), channel_id=1, source_target_pairs={{0,2},{16,18}} | collective-permute-start | bytes 2359304 | tf_op jit(solution)/shard_map/ppermute | solution.py:502
  198.6 15.6 %collective-permute-start.20 = (f32[272,1024]{1,0:T(8,128)S(1)}, f32[272,1024]{1,0:T(8,128)S(1)}, u32[]{:S(2)}, u32[]{:S(2)}) collective-permute-start(f32[272,1024]{1,0:T(8,128)S(1)} %collective-permute-done.13.refs_4_.refs_12_.refs_9_), channel_id=1, source_target_pairs={{5,13},{10,2},{15,7},{21,29},{26,18},{31,23}} | collective-permute-start | bytes 3342344 | tf_op jit(solution)/shard_map/ppermute | solution.py:502
  203.9 23.6 %collective-permute-start.17 = (f32[272,1024]{1,0:T(8,128)}, f32[272,1024]{1,0:T(8,128)S(1)}, u32[]{:S(2)}, u32[]{:S(2)}) collective-permute-start(f32[272,1024]{1,0:T(8,128)} %get-tuple-element.99), channel_id=1, source_target_pairs={{4,5},{8,9},{12,13},{5,6},{9,10},{13,14},{1,2},{6,7},{10,11},{14,1... | collective-permute-start | bytes 3342344 | tf_op jit(solution)/shard_map/ppermute | solution.py:502
  209.9 20.8 %collective-permute-start.18 = (f32[272,1024]{1,0:T(8,128)}, f32[272,1024]{1,0:T(8,128)S(1)}, u32[]{:S(2)}, u32[]{:S(2)}) collective-permute-start(f32[272,1024]{1,0:T(8,128)} %get-tuple-element.100), channel_id=1, source_target_pairs={{5,1},{1,9},{10,14},{14,6},{15,11},{11,3},{4,12},{21,17},{17,25},{... | collective-permute-start | bytes 3342344 | tf_op jit(solution)/shard_map/ppermute | solution.py:502
  211.2 2.9 collective-permute-start.19
  213.4 26.7 %collective-permute-start.21 = (f32[256,1024]{1,0:T(8,128)}, f32[256,1024]{1,0:T(8,128)S(1)}, u32[]{:S(2)}, u32[]{:S(2)}) collective-permute-start(f32[256,1024]{1,0:T(8,128)} %get-tuple-element.105.refs_10_), channel_id=1, source_target_pairs={{0,2},{16,18}} | collective-permute-start | bytes 3145736 | tf_op jit(solution)/shard_map/ppermute | solution.py:502
  235.4 19.9 %collective-permute-start.22 = (f32[272,1024]{1,0:T(8,128)}, f32[272,1024]{1,0:T(8,128)S(1)}, u32[]{:S(2)}, u32[]{:S(2)}) collective-permute-start(f32[272,1024]{1,0:T(8,128)} %get-tuple-element.106), channel_id=1, source_target_pairs={{4,5},{8,9},{12,13},{5,6},{9,10},{13,14},{1,2},{6,7},{10,11},{14,1... | collective-permute-start | bytes 3342344 | tf_op jit(solution)/shard_map/ppermute | solution.py:502
  237.3 25.4 %collective-permute-start.23 = (f32[272,1024]{1,0:T(8,128)}, f32[272,1024]{1,0:T(8,128)S(1)}, u32[]{:S(2)}, u32[]{:S(2)}) collective-permute-start(f32[272,1024]{1,0:T(8,128)} %get-tuple-element.107), channel_id=1, source_target_pairs={{5,1},{1,9},{10,14},{14,6},{15,11},{11,3},{4,12},{12,8},{21,17},{1... | collective-permute-start | bytes 3342344 | tf_op jit(solution)/shard_map/ppermute | solution.py:502
  238.6 24.1 %collective-permute-start.26 = (f32[272,1024]{1,0:T(8,128)}, f32[272,1024]{1,0:T(8,128)S(1)}, u32[]{:S(2)}, u32[]{:S(2)}) collective-permute-start(f32[272,1024]{1,0:T(8,128)} %copy-done.5), channel_id=1, source_target_pairs={{5,13},{10,2},{15,7},{21,29},{26,18},{31,23}} | collective-permute-start | bytes 3342344 | tf_op jit(solution)/shard_map/ppermute | solution.py:502
  239.3 1.5 collective-permute-start.25
  240.1 0.7 collective-permute-start.24
  267.6 6.1 %collective-permute-start.30 = (f32[256,768]{1,0:T(8,128)}, f32[256,768]{1,0:T(8,128)S(1)}, u32[]{:S(2)}, u32[]{:S(2)}) collective-permute-start(f32[256,768]{1,0:T(8,128)} %get-tuple-element.114.refs_10_), channel_id=1, source_target_pairs={{0,4},{1,5},{2,6},{3,7},{16,20},{17,21},{18,22},{19,23}} | collective-permute-start | bytes 2359304 | tf_op jit(solution)/shard_map/ppermute | solution.py:502
  268.3 71.9 %collective-permute-start.27 = (f32[272,1024]{1,0:T(8,128)}, f32[272,1024]{1,0:T(8,128)S(1)}, u32[]{:S(2)}, u32[]{:S(2)}) collective-permute-start(f32[272,1024]{1,0:T(8,128)} %get-tuple-element.111), channel_id=1, source_target_pairs={{4,5},{8,9},{12,13},{5,6},{9,10},{13,14},{1,2},{6,7},{10,11},{14,1... | collective-permute-start | bytes 3342344 | tf_op jit(solution)/shard_map/ppermute | solution.py:502
  270.9 69.3 %collective-permute-start.28 = (f32[272,1024]{1,0:T(8,128)}, f32[272,1024]{1,0:T(8,128)S(1)}, u32[]{:S(2)}, u32[]{:S(2)}) collective-permute-start(f32[272,1024]{1,0:T(8,128)} %get-tuple-element.112), channel_id=1, source_target_pairs={{5,1},{1,9},{10,14},{14,6},{15,11},{11,3},{4,12},{12,8},{21,17},{1... | collective-permute-start | bytes 3342344 | tf_op jit(solution)/shard_map/ppermute | solution.py:502
  272.2 68.0 %collective-permute-start.32 = (f32[272,1024]{1,0:T(8,128)}, f32[272,1024]{1,0:T(8,128)S(1)}, u32[]{:S(2)}, u32[]{:S(2)}) collective-permute-start(f32[272,1024]{1,0:T(8,128)} %copy-done.7), channel_id=1, source_target_pairs={{5,13},{10,2},{15,7},{21,29},{26,18},{31,23}} | collective-permute-start | bytes 3342344 | tf_op jit(solution)/shard_map/ppermute | solution.py:502
  273.0 2.1 collective-permute-start.29
  273.7 66.6 %copy-start.39 = (f32[256,768]{1,0:T(8,128)}, f32[256,768]{1,0:T(8,128)S(1)}, u32[]{:S(2)}) copy-start(f32[256,768]{1,0:T(8,128)S(1)} %collective-permute-done.30.refs_4_) | copy-start | bytes 2359300
  273.7 66.5 %collective-permute-start.31 = (f32[512,512]{1,0:T(8,128)}, f32[512,512]{1,0:T(8,128)S(1)}, u32[]{:S(2)}, u32[]{:S(2)}) collective-permute-start(f32[512,512]{1,0:T(8,128)} %get-tuple-element.115.refs_1_), channel_id=1, source_target_pairs={{0,8},{1,9},{2,10},{3,11},{4,12},{5,13},{6,14},{7,15},{16,24},{17,... | collective-permute-start | bytes 3145736 | tf_op jit(solution)/shard_map/ppermute | solution.py:502
  345.9 46.0 %collective-permute-start.33 = (f32[272,1024]{1,0:T(8,128)}, f32[272,1024]{1,0:T(8,128)S(1)}, u32[]{:S(2)}, u32[]{:S(2)}) collective-permute-start(f32[272,1024]{1,0:T(8,128)} %get-tuple-element.117), channel_id=1, source_target_pairs={{5,6},{9,10},{13,14},{1,2},{6,7},{10,11},{14,15},{2,3},{21,22},{25... | collective-permute-start | bytes 3342344 | tf_op jit(solution)/shard_map/ppermute | solution.py:502
  347.2 44.6 %collective-permute-start.34 = (f32[272,1024]{1,0:T(8,128)}, f32[272,1024]{1,0:T(8,128)S(1)}, u32[]{:S(2)}, u32[]{:S(2)}) collective-permute-start(f32[272,1024]{1,0:T(8,128)} %get-tuple-element.118), channel_id=1, source_target_pairs={{5,1},{1,9},{10,14},{14,6},{15,11},{11,3},{4,12},{12,8},{21,17},{1... | collective-permute-start | bytes 3342344 | tf_op jit(solution)/shard_map/ppermute | solution.py:502
  348.5 43.3 %collective-permute-start.37 = (f32[272,1024]{1,0:T(8,128)}, f32[272,1024]{1,0:T(8,128)S(1)}, u32[]{:S(2)}, u32[]{:S(2)}) collective-permute-start(f32[272,1024]{1,0:T(8,128)} %copy-done.20), channel_id=1, source_target_pairs={{5,13},{10,2},{15,7},{21,29},{26,18},{31,23}} | collective-permute-start | bytes 3342344 | tf_op jit(solution)/shard_map/ppermute | solution.py:502
  349.3 42.6 %collective-permute-start.35 = (f32[256,1024]{1,0:T(8,128)}, f32[256,1024]{1,0:T(8,128)S(1)}, u32[]{:S(2)}, u32[]{:S(2)}) collective-permute-start(f32[256,1024]{1,0:T(8,128)} %get-tuple-element.119.refs_8_), channel_id=1, source_target_pairs={{0,4},{1,5},{2,6},{3,7},{16,20},{17,21},{18,22},{19,23}} | collective-permute-start | bytes 3145736 | tf_op jit(solution)/shard_map/ppermute | solution.py:502
  350.0 41.8 %collective-permute-start.36 = (f32[256,768]{1,0:T(8,128)}, f32[256,768]{1,0:T(8,128)S(1)}, u32[]{:S(2)}, u32[]{:S(2)}) collective-permute-start(f32[256,768]{1,0:T(8,128)} %get-tuple-element.120.refs_3_), channel_id=1, source_target_pairs={{0,8},{1,9},{2,10},{3,11},{4,12},{5,13},{6,14},{7,15},{16,24},{17,... | collective-permute-start | bytes 2359304 | tf_op jit(solution)/shard_map/ppermute | solution.py:502
  398.1 50.1 %collective-permute-start.38 = (f32[272,1024]{1,0:T(8,128)}, f32[272,1024]{1,0:T(8,128)S(1)}, u32[]{:S(2)}, u32[]{:S(2)}) collective-permute-start(f32[272,1024]{1,0:T(8,128)} %get-tuple-element.122), channel_id=1, source_target_pairs={{1,2},{6,7},{10,11},{14,15},{2,3},{17,18},{22,23},{26,27},{30,31},... | collective-permute-start | bytes 3342344 | tf_op jit(solution)/shard_map/ppermute | solution.py:502
  398.9 49.4 %collective-permute-start.39 = (f32[272,1024]{1,0:T(8,128)}, f32[272,1024]{1,0:T(8,128)S(1)}, u32[]{:S(2)}, u32[]{:S(2)}) collective-permute-start(f32[272,1024]{1,0:T(8,128)} %get-tuple-element.123), channel_id=1, source_target_pairs={{1,9},{10,14},{14,6},{15,11},{11,3},{4,12},{12,8},{17,25},{26,30},... | collective-permute-start | bytes 3342344 | tf_op jit(solution)/shard_map/ppermute | solution.py:502
  400.2 48.1 %collective-permute-start.41 = (f32[272,1024]{1,0:T(8,128)}, f32[272,1024]{1,0:T(8,128)S(1)}, u32[]{:S(2)}, u32[]{:S(2)}) collective-permute-start(f32[272,1024]{1,0:T(8,128)} %copy-done.24), channel_id=1, source_target_pairs={{10,2},{15,7},{26,18},{31,23}} | collective-permute-start | bytes 3342344 | tf_op jit(solution)/shard_map/ppermute | solution.py:502
  400.9 47.4 %collective-permute-start.40 = (f32[256,1024]{1,0:T(8,128)}, f32[256,1024]{1,0:T(8,128)}, u32[]{:S(2)}, u32[]{:S(2)}) collective-permute-start(f32[256,1024]{1,0:T(8,128)} %get-tuple-element.124.refs_5_), channel_id=1, source_target_pairs={{0,8},{1,9},{2,10},{3,11},{4,12},{5,13},{6,14},{7,15},{16,24},{17,... | collective-permute-start | bytes 3145736 | tf_op jit(solution)/shard_map/ppermute | solution.py:502
  454.2 22.9 %collective-permute-start.42 = (f32[272,1024]{1,0:T(8,128)}, f32[272,1024]{1,0:T(8,128)S(1)}, u32[]{:S(2)}, u32[]{:S(2)}) collective-permute-start(f32[272,1024]{1,0:T(8,128)} %get-tuple-element.126), channel_id=1, source_target_pairs={{2,3},{18,19}} | collective-permute-start | bytes 3342344 | tf_op jit(solution)/shard_map/ppermute | solution.py:502
  454.9 22.2 %collective-permute-start.43 = (f32[272,1024]{1,0:T(8,128)}, f32[272,1024]{1,0:T(8,128)S(1)}, u32[]{:S(2)}, u32[]{:S(2)}) collective-permute-start(f32[272,1024]{1,0:T(8,128)} %get-tuple-element.127), channel_id=1, source_target_pairs={{14,6},{15,11},{11,3},{12,8},{30,22},{31,27},{27,19},{28,24}} | collective-permute-start | bytes 3342344 | tf_op jit(solution)/shard_map/ppermute | solution.py:502
  455.7 21.5 %collective-permute-start.44 = (f32[272,1024]{1,0:T(8,128)}, f32[272,1024]{1,0:T(8,128)S(1)}, u32[]{:S(2)}, u32[]{:S(2)}) collective-permute-start(f32[272,1024]{1,0:T(8,128)} %copy-done.27), channel_id=1, source_target_pairs={{15,7},{31,23}} | collective-permute-start | bytes 3342344 | tf_op jit(solution)/shard_map/ppermute | solution.py:502
  480.8 42.9 %collective-permute-start.45 = (f32[272,1024]{1,0:T(8,128)}, f32[272,1024]{1,0:T(8,128)S(1)}, u32[]{:S(2)}, u32[]{:S(2)}) collective-permute-start(f32[272,1024]{1,0:T(8,128)} %get-tuple-element.129), channel_id=1, source_target_pairs={{11,3},{27,19}} | collective-permute-start | bytes 3342344 | tf_op jit(solution)/shard_map/ppermute | solution.py:502
  (41 other events, 243.9 us)
